TPU v7x, 512 devices: a whole 4x4x16 slice. The times are simulated.
512 devices in a mesh: leaf: 32 (over z, core), front: 16 (over x, y).
Axes of the slice: x: 4, y: 4, z: 16, core: 2. Of those that a mesh axis runs over, the one named last changes fastest.
Arguments:
- rhs: bfloat16 [4, 196608, 256], P(None, ('leaf', 'front')), may hold values from -6 to 6
- dinv: bfloat16 [4, 196608, 384], P(None, ('leaf', 'front'))
- u_factor: bfloat16 [3, 196608, 128], P(None, ('leaf', 'front')), may hold values from -0.5 to 0.5
- v_factor: bfloat16 [3, 196608, 128], P(None, ('leaf', 'front')), may hold values from -0.02734375 to 0.02734375
- rank_sizes: int32 [3], replicated, may hold values from 64 to 128, as said below
- resid: float32 [32768, 256], P(('leaf', 'front')), may hold values from -6 to 6
- dest_front: int32 [32768, 1], P(('leaf', 'front')), may hold values from 0 to 15; in each aligned block of 64 rows (0 to 63, 64 to 127, ...) at most 8 rows name the same one
- dest_row: int32 [32768], P(('leaf', 'front')), may hold values from 0 to 383
- live_count: int32 [512], P(('leaf', 'front')), may hold values from 32 to 64, as said below
Outputs:
- solved: float32 [4, 196608, 256], P(None, ('leaf', 'front'))
Inputs may be any that keep to these rules, and one draw needn't show every extreme that they name: `rank_sizes`: each coupling's rank is at most 128, and some coupling has rank 128. `live_count`: some device has all 64 slots live. `dest_front`: among the slots of one device at most 8 name the same front index, live or not.
All inputs are finite; a program needn't handle non-finite values.
Results may differ from a plain program's by a relative error of at most 0.0003.
Values sent between devices are 32-bit elements; how exact they have to be, the bound alone decides.
No kernel may reach another device: no remote copies, remote signals or barrier semaphores. Data moves between devices by JAX's collectives and lax.ppermute only.
A program may use at most 64 MiB of HBM per device.

v0:
```python
import jax
import jax.numpy as jnp
from jax import lax
from jax.sharding import PartitionSpec as P


def partner(value, axis, stride):
    mask = 2**stride
    pairs = [(source, source ^ mask) for source in range(lax.axis_size(axis))]
    return lax.ppermute(value, axis, pairs)


def apply_block(block, vector_field):
    return jnp.dot(
        block.astype(jnp.float32),
        vector_field,
        precision=lax.Precision.HIGHEST,
        preferred_element_type=jnp.float32,
    )


def rank_space(factor, vector_field):
    return lax.dot_general(
        factor.astype(jnp.float32),
        vector_field,
        (((0,), (0,)), ((), ())),
        precision=lax.Precision.HIGHEST,
        preferred_element_type=jnp.float32,
    )


def expand_rank(factor, coupled):
    return jnp.dot(
        factor.astype(jnp.float32),
        coupled,
        precision=lax.Precision.HIGHEST,
        preferred_element_type=jnp.float32,
    )


def group_total(partial_value, coupling):
    leaf_devs = lax.axis_size("leaf")
    leaf_bits = leaf_devs.bit_length() - 1
    summed = lax.psum(partial_value, "front")
    for bit_index in range(leaf_bits - coupling):
        summed = summed + partner(summed, "leaf", bit_index)
    return summed


def per_device(rhs, dinv, u_factor, v_factor, rank_sizes, resid, dest_front, dest_row, live_count):
    levels = rhs.shape[0]
    rows_dev = rhs.shape[1]
    shots = rhs.shape[2]
    rank_cols = u_factor.shape[2]
    recv_rows = resid.shape[0]
    front_devs = lax.axis_size("front")
    live_slots = (jnp.arange(recv_rows) < live_count[0]).astype(jnp.float32)
    values = resid * live_slots[:, None]
    capacity = max(2, 2 * recv_rows // front_devs)
    onehot = (dest_front == jnp.arange(front_devs)[None, :]).astype(jnp.int32)
    before = jnp.cumsum(onehot, axis=0) - onehot
    position = jnp.sum(before * onehot, axis=1)
    slot_index = dest_front[:, 0] * capacity + position
    placement = slot_index[None, :] == jnp.arange(front_devs * capacity)[:, None]
    packed = jnp.dot(
        placement.astype(jnp.float32),
        values,
        precision=lax.Precision.HIGHEST,
        preferred_element_type=jnp.float32,
    )
    packed = packed.reshape(front_devs, capacity, shots)
    packed_rows = jnp.sum(jnp.where(placement, dest_row[None, :] + 1, 0), axis=1)
    packed_rows = packed_rows.reshape(front_devs, capacity)
    got_values, got_rows = (
        lax.all_to_all(packed, "front", split_axis=0, concat_axis=0, tiled=True),
        lax.all_to_all(packed_rows, "front", split_axis=0, concat_axis=0, tiled=True),
    )
    selector = (got_rows.reshape(-1)[None, :] - 1 == jnp.arange(rows_dev)[:, None]).astype(
        jnp.float32
    )
    sources = jnp.dot(
        selector,
        got_values.reshape(-1, shots),
        precision=lax.Precision.HIGHEST,
        preferred_element_type=jnp.float32,
    )
    rank_masks = []
    for coupling in range(levels - 1):
        rank_masks.append(
            (jnp.arange(rank_cols) < rank_sizes[coupling]).astype(jnp.float32)[:, None]
        )
    forward = [None] * levels
    forward[levels - 1] = apply_block(
        dinv[levels - 1], rhs[levels - 1].astype(jnp.float32) + sources
    )
    for coupling in range(levels - 2, -1, -1):
        partial_value = rank_space(v_factor[coupling], forward[coupling + 1])
        coupled = group_total(partial_value, coupling) * rank_masks[coupling]
        reduced = rhs[coupling].astype(jnp.float32) - expand_rank(u_factor[coupling], coupled)
        forward[coupling] = apply_block(dinv[coupling], reduced)
    solved = [forward[0]]
    for coupling in range(levels - 1):
        partial_value = rank_space(u_factor[coupling], solved[coupling])
        dual = group_total(partial_value, coupling) * rank_masks[coupling]
        update = apply_block(dinv[coupling + 1], expand_rank(v_factor[coupling], dual))
        solved.append(forward[coupling + 1] - update)
    return jnp.stack(solved)


def solution(mesh):
    in_specs = (
        P(None, ("leaf", "front"), None),
        P(None, ("leaf", "front"), None),
        P(None, ("leaf", "front"), None),
        P(None, ("leaf", "front"), None),
        P(),
        P(("leaf", "front"), None),
        P(("leaf", "front"), None),
        P(("leaf", "front")),
        P(("leaf", "front")),
    )
    out_specs = P(None, ("leaf", "front"), None)
    return jax.shard_map(
        per_device, mesh=mesh, in_specs=in_specs, out_specs=out_specs, check_vma=False
    )
```

profile of v0, /device:TPU:1, one launch (start us, length us, event | category | flops | bytes accessed | tf_op | source)
XLA Modules:
  0.0 975.4 jit_solution(3027305927270271886)
XLA Ops:
  9.8 7.6 all-to-all-start
  27.5 6.5 all-to-all-done.1
  37.2 115.1 %all-reduce.7.cloned.1.call-done = f32[128,256]{0,1:T(8,128)} async-done(((f32[128,256]{0,1:T(8,128)}), f32[128,256]{0,1:T(8,128)}) %all-reduce.7.cloned.1.call-update) | async-done | bytes 131088 | tf_op jit(solution)/shard_map/psum | solution.py:44
  178.1 112.0 %all-reduce.9.cloned.1.call-done = f32[128,256]{0,1:T(8,128)} async-done(((f32[128,256]{0,1:T(8,128)}), f32[128,256]{0,1:T(8,128)}) %all-reduce.9.cloned.1.call-update) | async-done | bytes 131088 | tf_op jit(solution)/shard_map/psum | solution.py:44
  307.1 5.8 collective-permute-done.5
  312.9 7.4 collective-permute-start.6
  321.1 9.8 %collective-permute-done.6 = f32[128,256]{0,1:T(8,128)} collective-permute-done((f32[128,256]{0,1:T(8,128)S(1)}, f32[128,256]{0,1:T(8,128)}, u32[]{:S(2)}, u32[]{:S(2)}) %collective-permute-start.6) | collective-permute-done | bytes 131104 | tf_op jit(solution)/shard_map/ppermute | solution.py:10
  333.7 110.8 %all-reduce.11.cloned.1.call-done = f32[128,256]{0,1:T(8,128)} async-done(((f32[128,256]{0,1:T(8,128)}), f32[128,256]{0,1:T(8,128)}) %all-reduce.11.cloned.1.call-update) | async-done | bytes 131088 | tf_op jit(solution)/shard_map/psum | solution.py:44
  461.5 5.8 collective-permute-done.9
  467.3 7.4 collective-permute-start.10
  474.7 10.5 %collective-permute-done.10 = f32[128,256]{0,1:T(8,128)S(1)} collective-permute-done((f32[128,256]{0,1:T(8,128)S(1)}, f32[128,256]{0,1:T(8,128)S(1)}, u32[]{:S(2)}, u32[]{:S(2)}) %collective-permute-start.10) | collective-permute-done | bytes 131104 | tf_op jit(solution)/shard_map/ppermute | solution.py:10
  485.9 12.4 %collective-permute-start.11 = (f32[128,256]{0,1:T(8,128)}, f32[128,256]{0,1:T(8,128)}, u32[]{:S(2)}, u32[]{:S(2)}) collective-permute-start(f32[128,256]{0,1:T(8,128)} %add.122), channel_id=1, source_target_pairs={{0,256},{16,272},{32,288},{48,304},{64,320},{80,336},{96,352},{112... | collective-permute-start | bytes 393224 | tf_op jit(solution)/shard_map/ppermute | solution.py:10
  499.1 11.2 %collective-permute-done.11 = f32[128,256]{0,1:T(8,128)} collective-permute-done((f32[128,256]{0,1:T(8,128)}, f32[128,256]{0,1:T(8,128)}, u32[]{:S(2)}, u32[]{:S(2)}) %collective-permute-start.11) | collective-permute-done | bytes 131104 | tf_op jit(solution)/shard_map/ppermute | solution.py:10
  513.2 104.0 %all-reduce.13.cloned.1.call-done = f32[128,256]{0,1:T(8,128)} async-done(((f32[128,256]{0,1:T(8,128)}), f32[128,256]{0,1:T(8,128)}) %all-reduce.13.cloned.1.call-update) | async-done | bytes 131088 | tf_op jit(solution)/shard_map/psum | solution.py:44
  634.2 5.8 collective-permute-done.14
  640.0 7.4 collective-permute-start.15
  647.4 10.5 %collective-permute-done.15 = f32[128,256]{0,1:T(8,128)S(1)} collective-permute-done((f32[128,256]{0,1:T(8,128)S(1)}, f32[128,256]{0,1:T(8,128)S(1)}, u32[]{:S(2)}, u32[]{:S(2)}) %collective-permute-start.15) | collective-permute-done | bytes 131104 | tf_op jit(solution)/shard_map/ppermute | solution.py:10
  657.9 12.4 %collective-permute-start.16 = (f32[128,256]{0,1:T(8,128)S(1)}, f32[128,256]{0,1:T(8,128)S(1)}, u32[]{:S(2)}, u32[]{:S(2)}) collective-permute-start(f32[128,256]{0,1:T(8,128)S(1)} %add.127), channel_id=1, source_target_pairs={{0,256},{16,272},{32,288},{48,304},{64,320},{80,336},{96,352},{112... | collective-permute-start | bytes 393224 | tf_op jit(solution)/shard_map/ppermute | solution.py:10
  670.4 11.7 %collective-permute-done.16 = f32[128,256]{0,1:T(8,128)S(1)} collective-permute-done((f32[128,256]{0,1:T(8,128)S(1)}, f32[128,256]{0,1:T(8,128)S(1)}, u32[]{:S(2)}, u32[]{:S(2)}) %collective-permute-start.16) | collective-permute-done | bytes 131104 | tf_op jit(solution)/shard_map/ppermute | solution.py:10
  684.0 104.0 %all-reduce.15.cloned.1.call-done = f32[128,256]{0,1:T(8,128)} async-done(((f32[128,256]{0,1:T(8,128)}), f32[128,256]{0,1:T(8,128)}) %all-reduce.15.cloned.1.call-update) | async-done | bytes 131088 | tf_op jit(solution)/shard_map/psum | solution.py:44
  805.0 5.8 collective-permute-done.19
  810.8 7.4 collective-permute-start.20
  818.2 10.5 %collective-permute-done.20 = f32[128,256]{0,1:T(8,128)S(1)} collective-permute-done((f32[128,256]{0,1:T(8,128)S(1)}, f32[128,256]{0,1:T(8,128)S(1)}, u32[]{:S(2)}, u32[]{:S(2)}) %collective-permute-start.20) | collective-permute-done | bytes 131104 | tf_op jit(solution)/shard_map/ppermute | solution.py:10
  831.4 110.8 %all-reduce.17.cloned.1.call-done = f32[128,256]{0,1:T(8,128)} async-done(((f32[128,256]{0,1:T(8,128)}), f32[128,256]{0,1:T(8,128)}) %all-reduce.17.cloned.1.call-update) | async-done | bytes 131088 | tf_op jit(solution)/shard_map/psum | solution.py:44
  (118 shorter events, 148.4 us)
Async XLA Ops:
  9.8 14.0 %all-to-all-start = ((s32[16,1,8]{2,1,0:T(1,128)}), s32[16,1,8]{2,1,0:T(1,128)S(1)}, u32[]{:S(2)}, u32[]{:S(2)}) async-start(s32[16,1,8]{2,1,0:T(1,128)} %bitcast.5), calls=%async_computation | async-start | bytes 16384 | tf_op jit(solution)/shard_map/all_to_all | solution.py:76
  23.8 10.2 %all-to-all-start.1 = ((f32[16,8,256]{2,1,0:T(8,128)}), f32[16,8,256]{2,1,0:T(8,128)S(1)}, u32[]{:S(2)}, u32[]{:S(2)}) async-start(f32[16,8,256]{2,1,0:T(8,128)} %convolution_bitcast_fusion.9), calls=%async_computation.1 | async-start | bytes 262144 | tf_op jit(solution)/shard_map/all_to_all | solution.py:75
  27.3 125.0 %all-reduce.7.cloned.1.call-start = ((), (), s32[]{:S(2)}) async-start(), calls=%async_computation.2 | async-start | bytes 262144 | tf_op jit(solution)/shard_map/psum | solution.py:44
  37.1 252.9 %all-reduce.9.cloned.1.call-start = ((), (), s32[]{:S(2)}) async-start(), calls=%async_computation.3 | async-start | bytes 262144 | tf_op jit(solution)/shard_map/psum | solution.py:44
  158.5 6.6 collective-permute-start.1
  165.2 10.1 %collective-permute-start.2 = (f32[128,256]{0,1:T(8,128)S(1)}, f32[128,256]{0,1:T(8,128)}, u32[]{:S(2)}, u32[]{:S(2)}) collective-permute-start(f32[128,256]{0,1:T(8,128)S(1)} %add.113), channel_id=1, source_target_pairs={{0,64},{16,80},{32,96},{48,112},{64,0},{80,16},{96,32},{112,48},{1... | collective-permute-start | bytes 393224 | tf_op jit(solution)/shard_map/ppermute | solution.py:10
  178.0 266.5 %all-reduce.11.cloned.1.call-start = ((), (), s32[]{:S(2)}) async-start(), calls=%async_computation.4 | async-start | bytes 262144 | tf_op jit(solution)/shard_map/psum | solution.py:44
  296.2 6.6 collective-permute-start.4
  302.9 10.0 %collective-permute-start.5 = (f32[128,256]{0,1:T(8,128)S(1)}, f32[128,256]{0,1:T(8,128)S(1)}, u32[]{:S(2)}, u32[]{:S(2)}) collective-permute-start(f32[128,256]{0,1:T(8,128)S(1)} %add.116), channel_id=1, source_target_pairs={{0,64},{16,80},{32,96},{48,112},{64,0},{80,16},{96,32},{112,48},{1... | collective-permute-start | bytes 393224 | tf_op jit(solution)/shard_map/ppermute | solution.py:10
  312.9 18.0 %collective-permute-start.6 = (f32[128,256]{0,1:T(8,128)S(1)}, f32[128,256]{0,1:T(8,128)}, u32[]{:S(2)}, u32[]{:S(2)}) collective-permute-start(f32[128,256]{0,1:T(8,128)S(1)} %add.117), channel_id=1, source_target_pairs={{0,128},{16,144},{32,160},{48,176},{64,192},{80,208},{96,224},{112... | collective-permute-start | bytes 393224 | tf_op jit(solution)/shard_map/ppermute | solution.py:10
  333.7 283.5 %all-reduce.13.cloned.1.call-start = ((), (), s32[]{:S(2)}) async-start(), calls=%async_computation.5 | async-start | bytes 262144 | tf_op jit(solution)/shard_map/psum | solution.py:44
  450.7 6.6 collective-permute-start.8
  457.4 10.0 %collective-permute-start.9 = (f32[128,256]{0,1:T(8,128)S(1)}, f32[128,256]{0,1:T(8,128)S(1)}, u32[]{:S(2)}, u32[]{:S(2)}) collective-permute-start(f32[128,256]{0,1:T(8,128)S(1)} %add.120), channel_id=1, source_target_pairs={{0,64},{16,80},{32,96},{48,112},{64,0},{80,16},{96,32},{112,48},{1... | collective-permute-start | bytes 393224 | tf_op jit(solution)/shard_map/ppermute | solution.py:10
  467.3 17.9 %collective-permute-start.10 = (f32[128,256]{0,1:T(8,128)S(1)}, f32[128,256]{0,1:T(8,128)S(1)}, u32[]{:S(2)}, u32[]{:S(2)}) collective-permute-start(f32[128,256]{0,1:T(8,128)S(1)} %add.121), channel_id=1, source_target_pairs={{0,128},{16,144},{32,160},{48,176},{64,192},{80,208},{96,224},{112... | collective-permute-start | bytes 393224 | tf_op jit(solution)/shard_map/ppermute | solution.py:10
  485.9 24.4 %collective-permute-start.11 = (f32[128,256]{0,1:T(8,128)}, f32[128,256]{0,1:T(8,128)}, u32[]{:S(2)}, u32[]{:S(2)}) collective-permute-start(f32[128,256]{0,1:T(8,128)} %add.122), channel_id=1, source_target_pairs={{0,256},{16,272},{32,288},{48,304},{64,320},{80,336},{96,352},{112... | collective-permute-start | bytes 393224 | tf_op jit(solution)/shard_map/ppermute | solution.py:10
  513.2 274.8 %all-reduce.15.cloned.1.call-start = ((), (), s32[]{:S(2)}) async-start(), calls=%async_computation.6 | async-start | bytes 262144 | tf_op jit(solution)/shard_map/psum | solution.py:44
  630.1 10.0 %collective-permute-start.14 = (f32[128,256]{0,1:T(8,128)S(1)}, f32[128,256]{0,1:T(8,128)S(1)}, u32[]{:S(2)}, u32[]{:S(2)}) collective-permute-start(f32[128,256]{0,1:T(8,128)S(1)} %add.125), channel_id=1, source_target_pairs={{0,64},{16,80},{32,96},{48,112},{64,0},{80,16},{96,32},{112,48},{1... | collective-permute-start | bytes 393224 | tf_op jit(solution)/shard_map/ppermute | solution.py:10
  640.0 17.9 %collective-permute-start.15 = (f32[128,256]{0,1:T(8,128)S(1)}, f32[128,256]{0,1:T(8,128)S(1)}, u32[]{:S(2)}, u32[]{:S(2)}) collective-permute-start(f32[128,256]{0,1:T(8,128)S(1)} %add.126), channel_id=1, source_target_pairs={{0,128},{16,144},{32,160},{48,176},{64,192},{80,208},{96,224},{112... | collective-permute-start | bytes 393224 | tf_op jit(solution)/shard_map/ppermute | solution.py:10
  657.9 24.1 %collective-permute-start.16 = (f32[128,256]{0,1:T(8,128)S(1)}, f32[128,256]{0,1:T(8,128)S(1)}, u32[]{:S(2)}, u32[]{:S(2)}) collective-permute-start(f32[128,256]{0,1:T(8,128)S(1)} %add.127), channel_id=1, source_target_pairs={{0,256},{16,272},{32,288},{48,304},{64,320},{80,336},{96,352},{112... | collective-permute-start | bytes 393224 | tf_op jit(solution)/shard_map/ppermute | solution.py:10
  684.0 258.3 %all-reduce.17.cloned.1.call-start = ((), (), s32[]{:S(2)}) async-start(), calls=%async_computation.7 | async-start | bytes 262144 | tf_op jit(solution)/shard_map/psum | solution.py:44
  800.8 10.0 %collective-permute-start.19 = (f32[128,256]{0,1:T(8,128)S(1)}, f32[128,256]{0,1:T(8,128)S(1)}, u32[]{:S(2)}, u32[]{:S(2)}) collective-permute-start(f32[128,256]{0,1:T(8,128)S(1)} %add.130), channel_id=1, source_target_pairs={{0,64},{16,80},{32,96},{48,112},{64,0},{80,16},{96,32},{112,48},{1... | collective-permute-start | bytes 393224 | tf_op jit(solution)/shard_map/ppermute | solution.py:10
  810.8 17.9 %collective-permute-start.20 = (f32[128,256]{0,1:T(8,128)S(1)}, f32[128,256]{0,1:T(8,128)S(1)}, u32[]{:S(2)}, u32[]{:S(2)}) collective-permute-start(f32[128,256]{0,1:T(8,128)S(1)} %add.131), channel_id=1, source_target_pairs={{0,128},{16,144},{32,160},{48,176},{64,192},{80,208},{96,224},{112... | collective-permute-start | bytes 393224 | tf_op jit(solution)/shard_map/ppermute | solution.py:10
  948.5 6.6 collective-permute-start.22
  955.1 10.0 %collective-permute-start.23 = (f32[128,256]{0,1:T(8,128)S(1)}, f32[128,256]{0,1:T(8,128)S(1)}, u32[]{:S(2)}, u32[]{:S(2)}) collective-permute-start(f32[128,256]{0,1:T(8,128)S(1)} %add.134), channel_id=1, source_target_pairs={{0,64},{16,80},{32,96},{48,112},{64,0},{80,16},{96,32},{112,48},{1... | collective-permute-start | bytes 393224 | tf_op jit(solution)/shard_map/ppermute | solution.py:10
  (15 other events, 673.1 us)
Sparse Core Ops, SparseCore 0:
  37.2 115.0 all-reduce.6
  178.1 111.8 all-reduce.8
  333.8 110.6 all-reduce.10
  513.3 103.8 all-reduce.12
  684.1 103.8 all-reduce.14
  831.6 110.6 all-reduce.16
where the time goes:
time: 977 us; the launch traced here: 975 us
  waiting for transfers between devices  792 us (81%)
  starting transfers between devices  135 us (14%)
  matrix products  19.5 us (2%)
  between operations  14.7 us (2%)
  other arithmetic  10.9 us (1%)
    psum x6, waiting for transfers between devices, group_total(): summed = lax.psum(partial_value, 'front')  657 us
    ppermute x24, waiting for transfers between devices, partner(): return lax.ppermute(value, axis, pairs)  124 us
    ppermute x24, starting transfers between devices, partner(): return lax.ppermute(value, axis, pairs)  123 us
  transfers between devices with their start and end apart: 32, of which 32 were waited for; matrix products, arithmetic and copies ran while one was open for 1% of the time, Pallas kernels for 0%

commit v1 on v0

v1 whole, which is shorter than its diff:
```python
import functools

import jax
import jax.numpy as jnp
from jax import lax
from jax.experimental import pallas as pl
from jax.experimental.pallas import tpu as pltpu
from jax.sharding import Mesh
from jax.sharding import PartitionSpec as P

F32 = jnp.float32
BF16 = jnp.bfloat16
LEVELS = 4
RANK = 128
SHOTS = 256
ROWS = 384
SLOTS = 8
FRONT = 16
HALF = RANK // 2
PART = 18
EARLY = 4 * PART
MESSAGE = EARLY + 16
SENT = 24
SPREAD = 32
ALL = ("zh", "zl", "core", "x", "y")

A2, R1V, A1, R0V, S0, B0, S1, B1, C1, S2, B2, C2, R2V = 0, 1, 3, 4, 6, 8, 9, 11, 12, 13, 15, 16, 17
G_R2V, G_A2, G_R1V, G_A1, G_R0V, G_S0, G_B0, G_S1, G_B1, G_C1, G_S2, G_B2, G_C2 = (
    0, 8, 12, 16, 18, 20, 22, 23, 25, 26, 27, 29, 30,
)


SOLVE = 16
BOTTOM = 53
WHOLE = 62


def params(mebibytes):
    return pltpu.CompilerParams(vmem_limit_bytes=int(mebibytes * 2**20))


VMEM = pl.BlockSpec(memory_space=pltpu.VMEM)
SMEM = pl.BlockSpec(memory_space=pltpu.SMEM)
HBM = pl.BlockSpec(memory_space=pltpu.HBM)


def split(value):
    high = value.astype(BF16)
    return high, (value - high.astype(F32)).astype(BF16)


def split3(value):
    high = value.astype(BF16)
    rest = value - high.astype(F32)
    mid = rest.astype(BF16)
    return high, mid, (rest - mid.astype(F32)).astype(BF16)


def mm(left, right):
    return jnp.dot(left, right, preferred_element_type=F32)


def mm_tn(left, right):
    return lax.dot_general(left, right, (((0,), (0,)), ((), ())), preferred_element_type=F32)


def mm_nt(left, right):
    return lax.dot_general(left, right, (((1,), (1,)), ((), ())), preferred_element_type=F32)


def mm3(left, right):
    left_high, left_low = split(left)
    right_high, right_low = split(right)
    return mm(left_high, right_high) + (mm(left_high, right_low) + mm(left_low, right_high))


def column(row_ref, count):
    diagonal = lax.broadcasted_iota(jnp.int32, (count, count), 0) == lax.broadcasted_iota(
        jnp.int32, (count, count), 1
    )
    return jnp.sum(jnp.where(diagonal, row_ref[...], 0), axis=1, keepdims=True)


def pack_kernel(
    core_ref, live_ref, resid_hbm, front_hbm, row_hbm, out_ref, core_out,
    resid_ref, front_ref, row_ref, sems,
):
    core_out[0] = core_ref[0]
    copies = [
        pltpu.make_async_copy(source, target, sems.at[index])
        for index, (source, target) in enumerate(
            ((front_hbm, front_ref), (row_hbm, row_ref), (resid_hbm, resid_ref))
        )
    ]
    for copy in copies:
        copy.start()
    recv = resid_ref.shape[0]
    live = lax.broadcasted_iota(jnp.int32, (recv, 1), 0) < live_ref[0]
    copies[0].wait()
    front = column(front_ref, recv)
    copies[1].wait()
    rows = jnp.where(live, column(row_ref, recv) + 1, 0)
    onehot = front == lax.broadcasted_iota(jnp.int32, (recv, FRONT), 1)
    earlier = lax.broadcasted_iota(jnp.int32, (recv, recv), 0) > lax.broadcasted_iota(
        jnp.int32, (recv, recv), 1
    )
    before = mm(earlier.astype(F32).astype(BF16), onehot.astype(F32).astype(BF16))
    position = jnp.sum(jnp.where(onehot, before, 0.0), axis=1, keepdims=True)
    slot = front * SLOTS + position.astype(jnp.int32)
    place = slot == lax.broadcasted_iota(jnp.int32, (recv, FRONT * SLOTS), 1)
    place = place.astype(F32).astype(BF16)
    copies[2].wait()
    high, mid, low = split3(jnp.where(live, resid_ref[...], 0.0))
    coarse = jnp.broadcast_to((rows & ~15).astype(F32), (recv, 128)).astype(BF16)
    fine = jnp.broadcast_to((rows & 15).astype(F32), (recv, 128)).astype(BF16)
    out_ref[:, :SHOTS] = mm_tn(place, high) + (mm_tn(place, mid) + mm_tn(place, low))
    out_ref[:, SHOTS:] = mm_tn(place, coarse) + mm_tn(place, fine)


def local_kernel(
    core_ref, rhs_hbm, dinv_hbm, u_hbm, v_hbm,
    own_hbm, bottom_hbm, up_hbm, down_hbm, mine_ref, send_ref,
    rhs_ref, dinv_ref, u_ref, v_ref, own_ref, up_ref, down_ref, wide_ref, narrow_ref,
    in_sems, out_sems,
):
    core = core_ref[0]
    loads = []
    for level in range(LEVELS):
        pairs = [(dinv_hbm, dinv_ref), (rhs_hbm, rhs_ref)]
        if level < LEVELS - 1:
            pairs += [(u_hbm, u_ref), (v_hbm, v_ref)]
        loads.append(
            [
                pltpu.make_async_copy(source.at[level], target.at[level], in_sems.at[level, index])
                for index, (source, target) in enumerate(pairs)
            ]
        )
        for copy in loads[-1]:
            copy.start()
    stores = []

    def keep(source, target):
        copy = pltpu.make_async_copy(source, target, out_sems.at[len(stores)])
        copy.start()
        stores.append(copy)

    def reduce(factor, pair):
        return mm_tn(factor, pair[0]) + mm_tn(factor, pair[1])

    def save(at, value):
        scratch = narrow_ref if value.shape[1] == 128 else wide_ref
        scratch[...] = value
        for piece in range(value.shape[1] // 128):
            rows = pl.ds(at + piece, HALF, stride=PART)
            lanes = slice(piece * 128, piece * 128 + 128)
            mine_ref[rows, :] = scratch[pl.ds(core * HALF, HALF), lanes]
            send_ref[rows, :] = scratch[pl.ds((1 - core) * HALF, HALF), lanes]

    mine_ref[...] = jnp.zeros_like(mine_ref)
    send_ref[...] = jnp.zeros_like(send_ref)
    for level in range(LEVELS):
        for copy in loads[level]:
            copy.wait()
        block = dinv_ref[level]
        own = mm(block, rhs_ref[level])
        own_ref[level] = own
        keep(own_ref.at[level], own_hbm.at[level] if level < LEVELS - 1 else bottom_hbm)
        if level > 0:
            down = split(mm(block, v_ref[level - 1]))
            down_ref[level - 1, 0], down_ref[level - 1, 1] = down
            keep(down_ref.at[level - 1], down_hbm.at[level - 1])
        if level == LEVELS - 1:
            continue
        up = split(mm(block, u_ref[level]))
        up_ref[level, 0], up_ref[level, 1] = up
        keep(up_ref.at[level], up_hbm.at[level])
        own = split(own)
        save((S0, S1, S2)[level], reduce(u_ref[level], own))
        save((B0, B1, B2)[level], reduce(u_ref[level], up))
        if level > 0:
            save((None, R0V, R1V)[level], reduce(v_ref[level - 1], own))
            save((None, A1, A2)[level], reduce(v_ref[level - 1], up))
            save((None, C1, C2)[level], reduce(u_ref[level], down))
    for copy in stores:
        copy.wait()


def bottom_kernel(
    got_ref, dinv_hbm, v_hbm, own_hbm, forward_ref, coupled_ref, dinv_ref, v_ref, own_ref, sems
):
    copies = [
        pltpu.make_async_copy(source, target, sems.at[index])
        for index, (source, target) in enumerate(
            (
                (dinv_hbm.at[LEVELS - 1], dinv_ref),
                (own_hbm, own_ref),
                (v_hbm.at[LEVELS - 2], v_ref),
            )
        )
    ]
    for copy in copies:
        copy.start()
    rowid = got_ref[:, SHOTS:]
    lane = lax.broadcasted_iota(jnp.int32, rowid.shape, 1).astype(F32) + 1.0
    select = jnp.concatenate(
        [(rowid == lane + 128.0 * part).astype(F32).astype(BF16) for part in range(ROWS // 128)],
        axis=1,
    )
    high, mid, low = split3(got_ref[:, :SHOTS])
    copies[0].wait()
    chosen = mm_nt(dinv_ref[...], select).astype(BF16)
    copies[1].wait()
    forward = own_ref[...] + (mm(chosen, high) + (mm(chosen, mid) + mm(chosen, low)))
    forward_ref[...] = forward
    high, low = split(forward)
    copies[2].wait()
    coupled_ref[...] = mm_tn(v_ref[...], high) + mm_tn(v_ref[...], low)


def message_kernel(coupled_ref, mine_ref, other_ref, out_ref):
    for front in range(FRONT):
        early = slice(front * EARLY, front * EARLY + EARLY)
        base = front * MESSAGE
        out_ref[base : base + EARLY, :] = mine_ref[early, :] + other_ref[early, :]
        for half in range(2):
            rows = slice(half * HALF + 4 * front, half * HALF + 4 * front + 4)
            for piece in range(2):
                at = base + EARLY + half * 8 + piece * 4
                out_ref[at : at + 4, :] = coupled_ref[rows, piece * 128 : piece * 128 + 128]


def total_kernel(core_ref, pieces_ref, out_ref):
    core = core_ref[0]
    total = pieces_ref[0]
    for index in range(1, FRONT):
        total = total + pieces_ref[index]
    out_ref[...] = jnp.zeros_like(out_ref)
    for zl in range(4):
        out_ref[zl * 2 + core, :R2V] = total[zl * PART : zl * PART + R2V]
        for half in range(2):
            for piece in range(2):
                at = EARLY + half * 8 + piece * 4 + zl
                out_ref[zl * 2 + half, R2V + piece : R2V + piece + 1] = total[at : at + 1]


def nodes_kernel(zh_ref, cross_ref, out_ref):
    zh = zh_ref[0]
    order = [zh, zh ^ 1, zh ^ 2, zh ^ 3]
    out_ref[...] = jnp.zeros_like(out_ref)
    for zl in range(4):
        nodes = [cross_ref[node * 4 + zl] for node in order]
        pair, other = nodes[0] + nodes[1], nodes[2] + nodes[3]
        total = pair + other
        for index, node in enumerate(nodes):
            out_ref[zl, G_R2V + 2 * index : G_R2V + 2 * index + 2] = node[R2V : R2V + 2]
            out_ref[zl, G_A2 + index : G_A2 + index + 1] = node[A2 : A2 + 1]
        for index, value in enumerate((pair, other)):
            out_ref[zl, G_R1V + 2 * index : G_R1V + 2 * index + 2] = value[R1V : R1V + 2]
            out_ref[zl, G_A1 + index : G_A1 + index + 1] = value[A1 : A1 + 1]
        out_ref[zl, G_R0V : G_R0V + 5] = total[R0V : R0V + 5]
        out_ref[zl, G_S1 : G_S1 + 4] = pair[S1 : S1 + 4]
        out_ref[zl, G_S2 : G_S2 + 4] = nodes[0][S2 : S2 + 4]


def solve_kernel(
    core_ref, rank_ref, mine_ref, other_ref, own_ref, forward_ref, up_ref, down_ref, out_hbm,
    out_ref, out_sems,
):
    stores = []

    def finish(level, value):
        out_ref[level] = value
        copy = pltpu.make_async_copy(out_ref.at[level], out_hbm.at[level], out_sems.at[level])
        copy.start()
        stores.append(copy)

    first = core_ref[0] == 0

    def block(at):
        mine = mine_ref[pl.ds(at, HALF, stride=SPREAD), :]
        other = other_ref[pl.ds(at, HALF, stride=SPREAD), :]
        return jnp.concatenate(
            [jnp.where(first, mine, other), jnp.where(first, other, mine)], axis=0
        )

    def wide(at):
        return jnp.concatenate([block(at), block(at + 1)], axis=1)

    def mask(coupling, value):
        keep = lax.broadcasted_iota(jnp.int32, value.shape, 0) < rank_ref[coupling]
        return jnp.where(keep, value, 0.0)

    def expand(pair_ref, index, value):
        high, low = split(value)
        left_high, left_low = pair_ref[index, 0], pair_ref[index, 1]
        return mm(left_high, high) + (mm(left_high, low) + mm(left_low, high))

    c2 = [mask(2, wide(G_R2V + 2 * node)) for node in range(4)]
    t1 = [mm3(block(G_A2 + node), c2[node]) for node in range(4)]
    c1 = [mask(1, wide(G_R1V + 2 * half) - (t1[2 * half] + t1[2 * half + 1])) for half in range(2)]
    t0 = [mm3(block(G_A1 + half), c1[half]) for half in range(2)]
    c0 = mask(0, wide(G_R0V) - (t0[0] + t0[1]))
    d0 = mask(0, wide(G_S0) - mm3(block(G_B0), c0))
    d1 = mask(1, wide(G_S1) - mm3(block(G_B1), c1[0]) - mm3(block(G_C1), d0))
    d2 = mask(2, wide(G_S2) - mm3(block(G_B2), c2[0]) - mm3(block(G_C2), d1))
    finish(0, own_ref[0] - expand(up_ref, 0, c0))
    finish(1, own_ref[1] - expand(up_ref, 1, c1[0]) - expand(down_ref, 0, d0))
    finish(2, own_ref[2] - expand(up_ref, 2, c2[0]) - expand(down_ref, 1, d1))
    finish(3, forward_ref[...] - expand(down_ref, 2, d2))
    for copy in stores:
        copy.wait()


def per_device(rhs, dinv, u_factor, v_factor, rank_sizes, resid, dest_front, dest_row, live_count):
    core = lax.axis_index("core").astype(jnp.int32).reshape(1)
    zh = lax.axis_index("zh").astype(jnp.int32).reshape(1)

    front = ("x", "y")
    swap = [(0, 1), (1, 0)]

    packed, core_after = pl.pallas_call(
        pack_kernel,
        out_shape=(
            jax.ShapeDtypeStruct((FRONT * SLOTS, SHOTS + 128), F32),
            jax.ShapeDtypeStruct((1,), jnp.int32),
        ),
        in_specs=[SMEM, SMEM, HBM, HBM, HBM],
        out_specs=(VMEM, SMEM),
        scratch_shapes=[
            pltpu.VMEM(resid.shape, F32),
            pltpu.VMEM((1, resid.shape[0]), jnp.int32),
            pltpu.VMEM((1, resid.shape[0]), jnp.int32),
            pltpu.SemaphoreType.DMA((3,)),
        ],
        compiler_params=params(WHOLE),
    )(core, live_count, resid, dest_front.reshape(1, -1), dest_row.reshape(1, -1))
    got = lax.all_to_all(
        packed.reshape(FRONT, SLOTS, SHOTS + 128), front, 0, 0, tiled=True
    ).reshape(FRONT * SLOTS, SHOTS + 128)

    pair = jax.ShapeDtypeStruct((LEVELS - 1, 2, ROWS, RANK), BF16)
    early = jax.ShapeDtypeStruct((HALF * PART, 128), F32)
    own, bottom, up, down, mine, send = pl.pallas_call(
        local_kernel,
        out_shape=(
            jax.ShapeDtypeStruct((LEVELS - 1, ROWS, SHOTS), F32),
            jax.ShapeDtypeStruct((ROWS, SHOTS), F32),
            pair,
            pair,
            early,
            early,
        ),
        in_specs=[SMEM] + [HBM] * 4,
        out_specs=(HBM,) * 4 + (VMEM,) * 2,
        scratch_shapes=[
            pltpu.VMEM(rhs.shape, BF16),
            pltpu.VMEM(dinv.shape, BF16),
            pltpu.VMEM(u_factor.shape, BF16),
            pltpu.VMEM(v_factor.shape, BF16),
            pltpu.VMEM((LEVELS, ROWS, SHOTS), F32),
            pltpu.VMEM(pair.shape, BF16),
            pltpu.VMEM(pair.shape, BF16),
            pltpu.VMEM((RANK, SHOTS), F32),
            pltpu.VMEM((RANK, RANK), F32),
            pltpu.SemaphoreType.DMA((LEVELS, 4)),
            pltpu.SemaphoreType.DMA((10,)),
        ],
        compiler_params=params(WHOLE),
        cost_estimate=pl.CostEstimate(
            flops=2_000_000_000, bytes_accessed=8_000_000, transcendentals=0
        ),
    )(core_after, rhs, dinv, u_factor, v_factor)
    got, send = lax.optimization_barrier((got, send))
    other = lax.ppermute(send, "core", swap)

    forward, coupled = pl.pallas_call(
        bottom_kernel,
        out_shape=(
            jax.ShapeDtypeStruct((ROWS, SHOTS), F32),
            jax.ShapeDtypeStruct((RANK, SHOTS), F32),
        ),
        in_specs=[VMEM] + [HBM] * 3,
        out_specs=(VMEM, VMEM),
        scratch_shapes=[
            pltpu.VMEM((ROWS, ROWS), BF16),
            pltpu.VMEM((ROWS, RANK), BF16),
            pltpu.VMEM((ROWS, SHOTS), F32),
            pltpu.SemaphoreType.DMA((3,)),
        ],
        compiler_params=params(BOTTOM),
    )(got, dinv, v_factor, bottom)
    message = pl.pallas_call(
        message_kernel,
        out_shape=jax.ShapeDtypeStruct((FRONT * MESSAGE, 128), F32),
        in_specs=[VMEM] * 3,
        out_specs=VMEM,
        compiler_params=params(4),
    )(coupled, mine, other)
    pieces = lax.all_to_all(message.reshape(FRONT, MESSAGE, 128), front, 0, 0, tiled=True)
    summed = pl.pallas_call(
        total_kernel,
        out_shape=jax.ShapeDtypeStruct((8, SENT, 128), F32),
        in_specs=[SMEM, VMEM],
        out_specs=VMEM,
        compiler_params=params(4),
    )(core, pieces)
    pieces = lax.all_to_all(summed, ("zl", "core"), 0, 0, tiled=True)
    reduced = jnp.sum(pieces, axis=0, keepdims=True)
    cross = lax.all_to_all(
        jnp.broadcast_to(reduced, (16, SENT, 128)), ("zh", "zl"), 0, 0, tiled=True
    )
    spread = pl.pallas_call(
        nodes_kernel,
        out_shape=jax.ShapeDtypeStruct((4, SPREAD, 128), F32),
        in_specs=[SMEM, VMEM],
        out_specs=VMEM,
        compiler_params=params(4),
    )(zh, cross)
    gathered = lax.all_to_all(
        jnp.broadcast_to(spread.reshape(1, 4 * SPREAD, 128), (FRONT, 4 * SPREAD, 128)),
        front, 0, 0, tiled=True,
    ).reshape(HALF * SPREAD, 128)
    other = lax.ppermute(gathered, "core", swap)

    return pl.pallas_call(
        solve_kernel,
        out_shape=jax.ShapeDtypeStruct((LEVELS, ROWS, SHOTS), F32),
        in_specs=[SMEM] * 2 + [VMEM] * 6,
        out_specs=HBM,
        scratch_shapes=[
            pltpu.VMEM((LEVELS, ROWS, SHOTS), F32),
            pltpu.SemaphoreType.DMA((LEVELS,)),
        ],
        compiler_params=params(SOLVE),
    )(core, rank_sizes, gathered, other, own, forward, up, down)


def solution(mesh):
    grid = Mesh(mesh.devices.reshape(4, 4, 2, 4, 4), ALL)
    wide = P(None, ALL, None)
    return jax.shard_map(
        per_device,
        mesh=grid,
        in_specs=(wide, wide, wide, wide, P(), P(ALL, None), P(ALL, None), P(ALL), P(ALL)),
        out_specs=wide,
        check_vma=False,
    )
```

time: 977 us -> 112 us (0.11)
  waiting for transfers between devices: 792 us -> 15 us
  starting transfers between devices: 135 us -> 33.6 us
  blocking collectives: 0 us -> 44.5 us
  matrix products: 19.5 us -> 0 us
  Pallas kernels: 0 us -> 15.5 us
  between operations: 14.7 us -> 0.83 us
  other arithmetic: 10.9 us -> 0.01 us
    psum x6 -> x0, waiting for transfers between devices: 657 us -> none  [group_total(): summed = lax.psum(partial_value, 'front')]
    ppermute x24 -> x2, waiting for transfers between devices: 124 us -> 2.27 us  [the longest x1 2.26 us: per_device(): other = lax.ppermute(gathered, 'core', swap)]
    ppermute x24 -> x2, starting transfers between devices: 123 us -> 13.8 us  [the longest x1 7.95 us: per_device(): other = lax.ppermute(gathered, 'core', swap)]
    all_to_all x0 -> x3, blocking collectives: none -> 44.5 us  [the longest x1 18.3 us: per_device(): lax.all_to_all(message.reshape(FRONT, MESSAGE, 128), front, 0, 0, tiled=T...]
    dot_general x21 -> x0, matrix products: 19.5 us -> none  [the longest x6 6.55 us: expand_rank(): jnp.dot(factor.astype(jnp.float32), coupled, precision=lax.Precision.HIGH...]
    pallas_call x0 -> x7, Pallas kernels: none -> 15.5 us  [the longest x1 6.56 us: per_device(): pl.pallas_call(local_kernel, out_shape=(jax.ShapeDtypeStruct((LEVELS - 1,...]
  transfers between devices with their start and end apart: 32 -> 4, of which waited for: 32 -> 3; matrix products, arithmetic and copies ran while one was open for 1% -> 0% of each run, Pallas kernels for 0% -> 8%
where the time goes in v1:
time: 112 us; the launch traced here: 110 us
  blocking collectives  44.5 us (40%)
  starting transfers between devices  33.6 us (30%)
  Pallas kernels  15.5 us (14%)
  waiting for transfers between devices  15 us (13%)
    all_to_all x1, blocking collectives, per_device(): lax.all_to_all(message.reshape(FRONT, MESSAGE, 128), front, 0, 0, tiled=T...  18.3 us
    all_to_all x1, blocking collectives, per_device(): lax.all_to_all(jnp.broadcast_to(spread.reshape(1, 4 * SPREAD, 128), (FRON...  15.4 us
    all_to_all x1, waiting for transfers between devices, per_device(): lax.all_to_all(jnp.broadcast_to(reduced, (16, SENT, 128)), ('zh', 'zl'),...  12.4 us
    all_to_all x1, starting transfers between devices, per_device(): lax.all_to_all(jnp.broadcast_to(reduced, (16, SENT, 128)), ('zh', 'zl'),...  12.2 us
    all_to_all x1, blocking collectives, per_device(): pieces = lax.all_to_all(summed, ('zl', 'core'), 0, 0, tiled=True)  10.8 us
    ppermute x1, starting transfers between devices, per_device(): other = lax.ppermute(gathered, 'core', swap)  7.95 us
    all_to_all x1, starting transfers between devices, per_device(): lax.all_to_all(packed.reshape(FRONT, SLOTS, SHOTS + 128), front, 0, 0, ti...  7.6 us
    pallas_call x1, Pallas kernels, per_device(): pl.pallas_call(local_kernel, out_shape=(jax.ShapeDtypeStruct((LEVELS - 1,...  6.56 us
  transfers between devices with their start and end apart: 4, of which 3 were waited for; matrix products, arithmetic and copies ran while one was open for 0% of the time, Pallas kernels for 8%

profile of v1, /device:TPU:1, one launch (start us, length us, event | category | flops | bytes accessed | tf_op | source)
XLA Modules:
  0.0 110.2 jit_solution(11810934951520807873)
XLA Ops:
  0.7 1.9 %shard_map.91 = (f32[128,384]{1,0:T(8,128)}, s32[1]{0:T(128)}) custom-call(s32[1]{0:T(128)} %bitcast.core_ref, s32[1]{0:T(128)S(6)} %copy.10.live_ref, f32[64,256]{1,0:T(8,128)} %resid_hbm.1, s32[1,64]{1,0:T(1,128)} %bitcast.15, s32[1,64]{1,0:T(1,128)} %bitcast.16), custom_call_target="tpu_custom_call" | custom-call | tf_op jit(solution)/shard_map/pallas_call | solution.py:321
  2.6 7.6 %all-to-all-start = ((f32[16,8,384]{2,1,0:T(8,128)}), f32[16,8,384]{2,1,0:T(8,128)S(1)}, u32[]{:S(2)}, u32[]{:S(2)}) async-start(f32[16,8,384]{2,1,0:T(8,128)} %bitcast.14), calls=%async_computation | async-start | bytes 393216 | tf_op jit(solution)/shard_map/all_to_all | solution.py:337
  10.2 0.0 copy-start.5
  10.2 6.6 %shard_map.92 = (f32[3,384,256]{2,1,0:T(8,128)}, f32[384,256]{1,0:T(8,128)}, bf16[3,2,384,128]{3,2,1,0:T(8,128)(2,1)}, bf16[3,2,384,128]{3,2,1,0:T(8,128)(2,1)},...) custom-call(s32[1]{0:T(128)} %get-tuple-element.18.core_ref, bf16[4,384,256]{2,1,0:T(8,128)(2,1)} %rhs_hbm.1, ...), custom_call_target="tpu_custom_call" | custom-call | flops 2000000000 | bytes 8000000 | tf_op jit(solution)/shard_map/pallas_call | solution.py:343
  16.8 0.3 all-to-all-done
  17.1 5.8 %collective-permute-start = (f32[1152,128]{1,0:T(8,128)}, f32[1152,128]{1,0:T(8,128)S(1)}, u32[]{:S(2)}, u32[]{:S(2)}) collective-permute-start(f32[1152,128]{1,0:T(8,128)} %get-tuple-element.24), channel_id=1, source_target_pairs={{0,16},{16,0},{1,17},{17,1},{2,18},{18,2},{3,19},{19,3},{4,20},{20... | collective-permute-start | bytes 1769480 | tf_op jit(solution)/shard_map/ppermute | solution.py:374
  23.0 2.5 %shard_map.93 = (f32[384,256]{1,0:T(8,128)}, f32[128,256]{1,0:T(8,128)S(1)}) custom-call(f32[128,384]{1,0:T(8,128)S(1)} %bitcast.12, bf16[4,384,384]{2,1,0:T(8,128)(2,1)} %dinv_hbm.3, bf16[3,384,128]{2,1,0:T(8,128)(2,1)S(1)} %copy-done.5, f32[384,256]{1,0:T(8,128)} %get-tuple-element.21.own_hbm), custom_call_target="tpu_custom_call" | custom-call | tf_op jit(solution)/shard_map/pallas_call | solution.py:376
  25.4 0.0 collective-permute-done.other_ref
  25.5 0.1 shard_map.94
  25.6 18.3 %all_to_all.25.pieces_ref = f32[16,88,128]{2,1,0:T(8,128)S(1)} all-to-all(f32[16,88,128]{2,1,0:T(8,128)S(1)} %bitcast.11), channel_id=1, replica_groups=mesh['zh'=4,'zl'=4,'core'=2,'x'=4,'y'=4] {'x','y'}, dimensions={0} | all-to-all | bytes 1441792 | tf_op jit(solution)/shard_map/all_to_all | solution.py:399
  43.9 10.8 %all_to_all.26 = f32[8,24,128]{2,1,0:T(8,128)S(1)} all-to-all(f32[8,24,128]{2,1,0:T(8,128)S(1)} %shard_map.95), channel_id=1, replica_groups=mesh['zh'=4,'zl'=4,'core'=2,'x'=4,'y'=4] {'zl','core'}, dimensions={0} | all-to-all | bytes 196608 | tf_op jit(solution)/shard_map/all_to_all | solution.py:407
  54.7 0.7 broadcast_in_dim.6
  55.4 12.2 %all-to-all-start.3 = ((f32[16,24,128]{2,1,0:T(8,128)}), f32[16,24,128]{2,1,0:T(8,128)S(1)}, u32[]{:S(2)}, u32[]{:S(2)}) async-start(f32[16,24,128]{2,1,0:T(8,128)} %broadcast_in_dim.6), calls=%async_computation.3 | async-start | bytes 393216 | tf_op jit(solution)/shard_map/all_to_all | solution.py:409
  67.7 12.4 %all-to-all-done.3.cross_ref = f32[16,24,128]{2,1,0:T(8,128)S(1)} async-done(((f32[16,24,128]{2,1,0:T(8,128)}), f32[16,24,128]{2,1,0:T(8,128)S(1)}, u32[]{:S(2)}, u32[]{:S(2)}) %all-to-all-start.3) | async-done | bytes 196640 | tf_op jit(solution)/shard_map/all_to_all | solution.py:409
  80.1 0.1 broadcast_in_dim.15
  80.2 0.0 copy-start
  80.2 0.0 copy-start.1
  80.2 0.0 copy-start.6
  80.2 15.4 %all_to_all.27 = f32[16,128,128]{2,1,0:T(8,128)S(1)} all-to-all(f32[16,128,128]{2,1,0:T(8,128)S(1)} %broadcast_in_dim.15), channel_id=1, replica_groups=mesh['zh'=4,'zl'=4,'core'=2,'x'=4,'y'=4] {'x','y'}, dimensions={0} | all-to-all | bytes 2097152 | tf_op jit(solution)/shard_map/all_to_all | solution.py:419
  95.6 7.9 %collective-permute-start.1 = (f32[2048,128]{1,0:T(8,128)S(1)}, f32[2048,128]{1,0:T(8,128)S(1)}, u32[]{:S(2)}, u32[]{:S(2)}) collective-permute-start(f32[2048,128]{1,0:T(8,128)S(1)} %bitcast.9), channel_id=1, source_target_pairs={{0,16},{16,0},{1,17},{17,1},{2,18},{18,2},{3,19},{19,3},{4,20},{20... | collective-permute-start | bytes 3145736 | tf_op jit(solution)/shard_map/ppermute | solution.py:423
  103.5 2.3 %collective-permute-done.1.other_ref = f32[2048,128]{1,0:T(8,128)S(1)} collective-permute-done((f32[2048,128]{1,0:T(8,128)S(1)}, f32[2048,128]{1,0:T(8,128)S(1)}, u32[]{:S(2)}, u32[]{:S(2)}) %collective-permute-start.1) | collective-permute-done | bytes 1048608 | tf_op jit(solution)/shard_map/ppermute | solution.py:423
  105.8 0.0 copy-done.1
  105.8 0.0 copy-done.6
  105.8 4.4 %shard_map.97 = f32[4,384,256]{2,1,0:T(8,128)} custom-call(s32[1]{0:T(128)} %bitcast.core_ref, s32[3]{0:T(128)S(1)} %copy-done.6, f32[2048,128]{1,0:T(8,128)S(1)} %bitcast.10, f32[2048,128]{1,0:T(8,128)S(1)} %collective-permute-done.1.other_ref, f32[3,384,256]{2,1,0:T(8,128)S(1)} %copy-done, f32[384,256]{1,0:T(8,128)S(1)} %copy-done.4, ...), custom_call_target="tpu_custom_call" | custom-call | tf_op jit(solution)/shard_map/pallas_call | solution.py:425
  (11 shorter events, 0.1 us)
Async XLA Ops:
  2.6 14.5 %all-to-all-start = ((f32[16,8,384]{2,1,0:T(8,128)}), f32[16,8,384]{2,1,0:T(8,128)S(1)}, u32[]{:S(2)}, u32[]{:S(2)}) async-start(f32[16,8,384]{2,1,0:T(8,128)} %bitcast.14), calls=%async_computation | async-start | bytes 393216 | tf_op jit(solution)/shard_map/all_to_all | solution.py:337
  10.2 12.8 %copy-start.5 = (bf16[3,384,128]{2,1,0:T(8,128)(2,1)S(1)}, bf16[3,384,128]{2,1,0:T(8,128)(2,1)}, u32[]{:S(2)}) copy-start(bf16[3,384,128]{2,1,0:T(8,128)(2,1)} %v_hbm.3) | copy-start | bytes 884740
  16.8 8.7 %copy-start.3 = (f32[1152,128]{1,0:T(8,128)S(1)}, f32[1152,128]{1,0:T(8,128)}, u32[]{:S(2)}) copy-start(f32[1152,128]{1,0:T(8,128)} %get-tuple-element.23.mine_ref) | copy-start | bytes 1769476
  17.1 8.3 %collective-permute-start = (f32[1152,128]{1,0:T(8,128)}, f32[1152,128]{1,0:T(8,128)S(1)}, u32[]{:S(2)}, u32[]{:S(2)}) collective-permute-start(f32[1152,128]{1,0:T(8,128)} %get-tuple-element.24), channel_id=1, source_target_pairs={{0,16},{16,0},{1,17},{17,1},{2,18},{18,2},{3,19},{19,3},{4,20},{20... | collective-permute-start | bytes 1769480 | tf_op jit(solution)/shard_map/ppermute | solution.py:374
  55.4 24.6 %all-to-all-start.3 = ((f32[16,24,128]{2,1,0:T(8,128)}), f32[16,24,128]{2,1,0:T(8,128)S(1)}, u32[]{:S(2)}, u32[]{:S(2)}) async-start(f32[16,24,128]{2,1,0:T(8,128)} %broadcast_in_dim.6), calls=%async_computation.3 | async-start | bytes 393216 | tf_op jit(solution)/shard_map/all_to_all | solution.py:409
  80.1 25.8 %copy-start.2 = (bf16[3,2,384,128]{3,2,1,0:T(8,128)(2,1)S(1)}, bf16[3,2,384,128]{3,2,1,0:T(8,128)(2,1)}, u32[]{:S(2)}) copy-start(bf16[3,2,384,128]{3,2,1,0:T(8,128)(2,1)} %get-tuple-element.28.down_ref) | copy-start | bytes 1769476
  80.1 25.8 %copy-start.4 = (f32[384,256]{1,0:T(8,128)S(1)}, f32[384,256]{1,0:T(8,128)}, u32[]{:S(2)}) copy-start(f32[384,256]{1,0:T(8,128)} %get-tuple-element.26.forward_ref) | copy-start | bytes 1179652
  80.2 25.6 %copy-start = (f32[3,384,256]{2,1,0:T(8,128)S(1)}, f32[3,384,256]{2,1,0:T(8,128)}, u32[]{:S(2)}) copy-start(f32[3,384,256]{2,1,0:T(8,128)} %get-tuple-element.25.own_ref) | copy-start | bytes 3538948
  80.2 25.6 %copy-start.1 = (bf16[3,2,384,128]{3,2,1,0:T(8,128)(2,1)S(1)}, bf16[3,2,384,128]{3,2,1,0:T(8,128)(2,1)}, u32[]{:S(2)}) copy-start(bf16[3,2,384,128]{3,2,1,0:T(8,128)(2,1)} %get-tuple-element.27.up_ref) | copy-start | bytes 1769476
  80.2 25.6 %copy-start.6 = (s32[3]{0:T(128)S(1)}, s32[3]{0:T(128)}, u32[]{:S(2)}) copy-start(s32[3]{0:T(128)} %rank_ref.1) | copy-start | bytes 40
  95.6 10.2 %collective-permute-start.1 = (f32[2048,128]{1,0:T(8,128)S(1)}, f32[2048,128]{1,0:T(8,128)S(1)}, u32[]{:S(2)}, u32[]{:S(2)}) collective-permute-start(f32[2048,128]{1,0:T(8,128)S(1)} %bitcast.9), channel_id=1, source_target_pairs={{0,16},{16,0},{1,17},{17,1},{2,18},{18,2},{3,19},{19,3},{4,20},{20... | collective-permute-start | bytes 3145736 | tf_op jit(solution)/shard_map/ppermute | solution.py:423

commit v2 on v1

--- a/solution.py
+++ b/solution.py
@@ -20,18 +20,20 @@
 PART = 18
 EARLY = 4 * PART
 MESSAGE = EARLY + 16
-SENT = 24
+SENT = 32
+CROSS = 16
+NODE = 4
 SPREAD = 32
 ALL = ("zh", "zl", "core", "x", "y")
 
-A2, R1V, A1, R0V, S0, B0, S1, B1, C1, S2, B2, C2, R2V = 0, 1, 3, 4, 6, 8, 9, 11, 12, 13, 15, 16, 17
+A2, R1V, A1, R0V, S0, B0, S1, B1, C1, S2, B2, C2 = 0, 1, 3, 4, 6, 8, 9, 11, 12, 13, 15, 16
+R2V = S2
 G_R2V, G_A2, G_R1V, G_A1, G_R0V, G_S0, G_B0, G_S1, G_B1, G_C1, G_S2, G_B2, G_C2 = (
     0, 8, 12, 16, 18, 20, 22, 23, 25, 26, 27, 29, 30,
 )
 
 
 SOLVE = 16
-BOTTOM = 53
 WHOLE = 62
 
 
@@ -82,10 +84,8 @@
 
 
 def pack_kernel(
-    core_ref, live_ref, resid_hbm, front_hbm, row_hbm, out_ref, core_out,
-    resid_ref, front_ref, row_ref, sems,
+    live_ref, resid_hbm, front_hbm, row_hbm, out_ref, resid_ref, front_ref, row_ref, sems
 ):
-    core_out[0] = core_ref[0]
     copies = [
         pltpu.make_async_copy(source, target, sems.at[index])
         for index, (source, target) in enumerate(
@@ -118,17 +118,17 @@
 
 
 def local_kernel(
-    core_ref, rhs_hbm, dinv_hbm, u_hbm, v_hbm,
-    own_hbm, bottom_hbm, up_hbm, down_hbm, mine_ref, send_ref,
+    rhs_hbm, dinv_hbm, u_hbm, v_hbm,
+    own_hbm, up_hbm, down_hbm, mine_ref, send_ref,
     rhs_ref, dinv_ref, u_ref, v_ref, own_ref, up_ref, down_ref, wide_ref, narrow_ref,
     in_sems, out_sems,
 ):
-    core = core_ref[0]
+    core = lax.axis_index("core")
     loads = []
     for level in range(LEVELS):
-        pairs = [(dinv_hbm, dinv_ref), (rhs_hbm, rhs_ref)]
+        pairs = [(dinv_hbm, dinv_ref)]
         if level < LEVELS - 1:
-            pairs += [(u_hbm, u_ref), (v_hbm, v_ref)]
+            pairs += [(rhs_hbm, rhs_ref), (u_hbm, u_ref), (v_hbm, v_ref)]
         loads.append(
             [
                 pltpu.make_async_copy(source.at[level], target.at[level], in_sems.at[level, index])
@@ -162,15 +162,15 @@
         for copy in loads[level]:
             copy.wait()
         block = dinv_ref[level]
-        own = mm(block, rhs_ref[level])
-        own_ref[level] = own
-        keep(own_ref.at[level], own_hbm.at[level] if level < LEVELS - 1 else bottom_hbm)
         if level > 0:
             down = split(mm(block, v_ref[level - 1]))
             down_ref[level - 1, 0], down_ref[level - 1, 1] = down
             keep(down_ref.at[level - 1], down_hbm.at[level - 1])
         if level == LEVELS - 1:
             continue
+        own = mm(block, rhs_ref[level])
+        own_ref[level] = own
+        keep(own_ref.at[level], own_hbm.at[level])
         up = split(mm(block, u_ref[level]))
         up_ref[level, 0], up_ref[level, 1] = up
         keep(up_ref.at[level], up_hbm.at[level])
@@ -185,21 +185,7 @@
         copy.wait()
 
 
-def bottom_kernel(
-    got_ref, dinv_hbm, v_hbm, own_hbm, forward_ref, coupled_ref, dinv_ref, v_ref, own_ref, sems
-):
-    copies = [
-        pltpu.make_async_copy(source, target, sems.at[index])
-        for index, (source, target) in enumerate(
-            (
-                (dinv_hbm.at[LEVELS - 1], dinv_ref),
-                (own_hbm, own_ref),
-                (v_hbm.at[LEVELS - 2], v_ref),
-            )
-        )
-    ]
-    for copy in copies:
-        copy.start()
+def bottom_kernel(got_ref, dinv_ref, v_ref, rhs_ref, forward_ref, coupled_ref):
     rowid = got_ref[:, SHOTS:]
     lane = lax.broadcasted_iota(jnp.int32, rowid.shape, 1).astype(F32) + 1.0
     select = jnp.concatenate(
@@ -207,14 +193,13 @@
         axis=1,
     )
     high, mid, low = split3(got_ref[:, :SHOTS])
-    copies[0].wait()
-    chosen = mm_nt(dinv_ref[...], select).astype(BF16)
-    copies[1].wait()
-    forward = own_ref[...] + (mm(chosen, high) + (mm(chosen, mid) + mm(chosen, low)))
+    block = dinv_ref[LEVELS - 1]
+    chosen = mm_nt(block, select).astype(BF16)
+    forward = mm(block, rhs_ref[LEVELS - 1]) + (mm(chosen, high) + (mm(chosen, mid) + mm(chosen, low)))
     forward_ref[...] = forward
     high, low = split(forward)
-    copies[2].wait()
-    coupled_ref[...] = mm_tn(v_ref[...], high) + mm_tn(v_ref[...], low)
+    factor = v_ref[LEVELS - 2]
+    coupled_ref[...] = mm_tn(factor, high) + mm_tn(factor, low)
 
 
 def message_kernel(coupled_ref, mine_ref, other_ref, out_ref):
@@ -229,41 +214,56 @@
                 out_ref[at : at + 4, :] = coupled_ref[rows, piece * 128 : piece * 128 + 128]
 
 
-def total_kernel(core_ref, pieces_ref, out_ref):
-    core = core_ref[0]
+def total_kernel(pieces_ref, out_ref):
+    core = lax.axis_index("core")
     total = pieces_ref[0]
     for index in range(1, FRONT):
         total = total + pieces_ref[index]
     out_ref[...] = jnp.zeros_like(out_ref)
     for zl in range(4):
-        out_ref[zl * 2 + core, :R2V] = total[zl * PART : zl * PART + R2V]
+        out_ref[zl * 2 + core, :S2] = total[zl * PART : zl * PART + S2]
+        for other in range(4):
+            at = CROSS + NODE * other
+            out_ref[zl * 2 + core, at : at + NODE] = total[
+                other * PART + S2 : other * PART + S2 + NODE
+            ]
         for half in range(2):
             for piece in range(2):
                 at = EARLY + half * 8 + piece * 4 + zl
                 out_ref[zl * 2 + half, R2V + piece : R2V + piece + 1] = total[at : at + 1]
 
 
-def nodes_kernel(zh_ref, cross_ref, out_ref):
-    zh = zh_ref[0]
+def share_kernel(pieces_ref, cross_ref, node_ref):
+    total = pieces_ref[0]
+    for index in range(1, 8):
+        total = total + pieces_ref[index]
+    for index in range(16):
+        cross_ref[index] = total[:CROSS]
+    node_ref[...] = total[CROSS:]
+
+
+def nodes_kernel(cross_ref, node_ref, out_ref):
+    zh = lax.axis_index("zh")
     order = [zh, zh ^ 1, zh ^ 2, zh ^ 3]
-    out_ref[...] = jnp.zeros_like(out_ref)
     for zl in range(4):
         nodes = [cross_ref[node * 4 + zl] for node in order]
         pair, other = nodes[0] + nodes[1], nodes[2] + nodes[3]
         total = pair + other
-        for index, node in enumerate(nodes):
-            out_ref[zl, G_R2V + 2 * index : G_R2V + 2 * index + 2] = node[R2V : R2V + 2]
-            out_ref[zl, G_A2 + index : G_A2 + index + 1] = node[A2 : A2 + 1]
-        for index, value in enumerate((pair, other)):
-            out_ref[zl, G_R1V + 2 * index : G_R1V + 2 * index + 2] = value[R1V : R1V + 2]
-            out_ref[zl, G_A1 + index : G_A1 + index + 1] = value[A1 : A1 + 1]
-        out_ref[zl, G_R0V : G_R0V + 5] = total[R0V : R0V + 5]
-        out_ref[zl, G_S1 : G_S1 + 4] = pair[S1 : S1 + 4]
-        out_ref[zl, G_S2 : G_S2 + 4] = nodes[0][S2 : S2 + 4]
+        spread = jnp.concatenate(
+            [node[R2V : R2V + 2] for node in nodes]
+            + [node[A2 : A2 + 1] for node in nodes]
+            + [value[R1V : R1V + 2] for value in (pair, other)]
+            + [value[A1 : A1 + 1] for value in (pair, other)]
+            + [total[R0V : R0V + 5], pair[S1 : S1 + 4]]
+            + [node_ref[NODE * zl : NODE * zl + NODE], jnp.zeros((1, 128), F32)],
+            axis=0,
+        )
+        for front in range(FRONT):
+            out_ref[front, zl * SPREAD : zl * SPREAD + SPREAD] = spread
 
 
 def solve_kernel(
-    core_ref, rank_ref, mine_ref, other_ref, own_ref, forward_ref, up_ref, down_ref, out_hbm,
+    rank_ref, mine_ref, other_ref, own_ref, forward_ref, up_ref, down_ref, out_hbm,
     out_ref, out_sems,
 ):
     stores = []
@@ -274,7 +274,7 @@
         copy.start()
         stores.append(copy)
 
-    first = core_ref[0] == 0
+    first = lax.axis_index("core") == 0
 
     def block(at):
         mine = mine_ref[pl.ds(at, HALF, stride=SPREAD), :]
@@ -287,7 +287,7 @@
         return jnp.concatenate([block(at), block(at + 1)], axis=1)
 
     def mask(coupling, value):
-        keep = lax.broadcasted_iota(jnp.int32, value.shape, 0) < rank_ref[coupling]
+        keep = lax.broadcasted_iota(jnp.int32, value.shape, 0) < rank_ref[:, coupling : coupling + 1]
         return jnp.where(keep, value, 0.0)
 
     def expand(pair_ref, index, value):
@@ -312,20 +312,15 @@
 
 
 def per_device(rhs, dinv, u_factor, v_factor, rank_sizes, resid, dest_front, dest_row, live_count):
-    core = lax.axis_index("core").astype(jnp.int32).reshape(1)
-    zh = lax.axis_index("zh").astype(jnp.int32).reshape(1)
 
     front = ("x", "y")
     swap = [(0, 1), (1, 0)]
 
-    packed, core_after = pl.pallas_call(
+    packed = pl.pallas_call(
         pack_kernel,
-        out_shape=(
-            jax.ShapeDtypeStruct((FRONT * SLOTS, SHOTS + 128), F32),
-            jax.ShapeDtypeStruct((1,), jnp.int32),
-        ),
-        in_specs=[SMEM, SMEM, HBM, HBM, HBM],
-        out_specs=(VMEM, SMEM),
+        out_shape=jax.ShapeDtypeStruct((FRONT * SLOTS, SHOTS + 128), F32),
+        in_specs=[SMEM, HBM, HBM, HBM],
+        out_specs=VMEM,
         scratch_shapes=[
             pltpu.VMEM(resid.shape, F32),
             pltpu.VMEM((1, resid.shape[0]), jnp.int32),
@@ -333,43 +328,43 @@
             pltpu.SemaphoreType.DMA((3,)),
         ],
         compiler_params=params(WHOLE),
-    )(core, live_count, resid, dest_front.reshape(1, -1), dest_row.reshape(1, -1))
+    )(live_count, resid, dest_front.reshape(1, -1), dest_row.reshape(1, -1))
+    packed, dinv_after = lax.optimization_barrier((packed, dinv))
     got = lax.all_to_all(
         packed.reshape(FRONT, SLOTS, SHOTS + 128), front, 0, 0, tiled=True
     ).reshape(FRONT * SLOTS, SHOTS + 128)
 
     pair = jax.ShapeDtypeStruct((LEVELS - 1, 2, ROWS, RANK), BF16)
     early = jax.ShapeDtypeStruct((HALF * PART, 128), F32)
-    own, bottom, up, down, mine, send = pl.pallas_call(
+    own, up, down, mine, send = pl.pallas_call(
         local_kernel,
         out_shape=(
             jax.ShapeDtypeStruct((LEVELS - 1, ROWS, SHOTS), F32),
-            jax.ShapeDtypeStruct((ROWS, SHOTS), F32),
             pair,
             pair,
             early,
             early,
         ),
-        in_specs=[SMEM] + [HBM] * 4,
-        out_specs=(HBM,) * 4 + (VMEM,) * 2,
+        in_specs=[HBM] * 4,
+        out_specs=(HBM,) * 3 + (VMEM,) * 2,
         scratch_shapes=[
             pltpu.VMEM(rhs.shape, BF16),
             pltpu.VMEM(dinv.shape, BF16),
             pltpu.VMEM(u_factor.shape, BF16),
             pltpu.VMEM(v_factor.shape, BF16),
-            pltpu.VMEM((LEVELS, ROWS, SHOTS), F32),
+            pltpu.VMEM((LEVELS - 1, ROWS, SHOTS), F32),
             pltpu.VMEM(pair.shape, BF16),
             pltpu.VMEM(pair.shape, BF16),
             pltpu.VMEM((RANK, SHOTS), F32),
             pltpu.VMEM((RANK, RANK), F32),
             pltpu.SemaphoreType.DMA((LEVELS, 4)),
-            pltpu.SemaphoreType.DMA((10,)),
+            pltpu.SemaphoreType.DMA((9,)),
         ],
         compiler_params=params(WHOLE),
         cost_estimate=pl.CostEstimate(
             flops=2_000_000_000, bytes_accessed=8_000_000, transcendentals=0
         ),
-    )(core_after, rhs, dinv, u_factor, v_factor)
+    )(rhs, dinv_after, u_factor, v_factor)
     got, send = lax.optimization_barrier((got, send))
     other = lax.ppermute(send, "core", swap)
 
@@ -379,16 +374,10 @@
             jax.ShapeDtypeStruct((ROWS, SHOTS), F32),
             jax.ShapeDtypeStruct((RANK, SHOTS), F32),
         ),
-        in_specs=[VMEM] + [HBM] * 3,
+        in_specs=[VMEM] * 4,
         out_specs=(VMEM, VMEM),
-        scratch_shapes=[
-            pltpu.VMEM((ROWS, ROWS), BF16),
-            pltpu.VMEM((ROWS, RANK), BF16),
-            pltpu.VMEM((ROWS, SHOTS), F32),
-            pltpu.SemaphoreType.DMA((3,)),
-        ],
-        compiler_params=params(BOTTOM),
-    )(got, dinv, v_factor, bottom)
+        compiler_params=params(8),
+    )(got, dinv, v_factor, rhs)
     message = pl.pallas_call(
         message_kernel,
         out_shape=jax.ShapeDtypeStruct((FRONT * MESSAGE, 128), F32),
@@ -400,39 +389,43 @@
     summed = pl.pallas_call(
         total_kernel,
         out_shape=jax.ShapeDtypeStruct((8, SENT, 128), F32),
-        in_specs=[SMEM, VMEM],
+        in_specs=[VMEM],
         out_specs=VMEM,
         compiler_params=params(4),
-    )(core, pieces)
+    )(pieces)
     pieces = lax.all_to_all(summed, ("zl", "core"), 0, 0, tiled=True)
-    reduced = jnp.sum(pieces, axis=0, keepdims=True)
-    cross = lax.all_to_all(
-        jnp.broadcast_to(reduced, (16, SENT, 128)), ("zh", "zl"), 0, 0, tiled=True
-    )
+    cross, node = pl.pallas_call(
+        share_kernel,
+        out_shape=(
+            jax.ShapeDtypeStruct((16, CROSS, 128), F32),
+            jax.ShapeDtypeStruct((4 * NODE, 128), F32),
+        ),
+        in_specs=[VMEM],
+        out_specs=(VMEM, VMEM),
+        compiler_params=params(4),
+    )(pieces)
+    cross = lax.all_to_all(cross, ("zh", "zl"), 0, 0, tiled=True)
     spread = pl.pallas_call(
         nodes_kernel,
-        out_shape=jax.ShapeDtypeStruct((4, SPREAD, 128), F32),
-        in_specs=[SMEM, VMEM],
+        out_shape=jax.ShapeDtypeStruct((FRONT, 4 * SPREAD, 128), F32),
+        in_specs=[VMEM, VMEM],
         out_specs=VMEM,
         compiler_params=params(4),
-    )(zh, cross)
-    gathered = lax.all_to_all(
-        jnp.broadcast_to(spread.reshape(1, 4 * SPREAD, 128), (FRONT, 4 * SPREAD, 128)),
-        front, 0, 0, tiled=True,
-    ).reshape(HALF * SPREAD, 128)
+    )(cross, node)
+    gathered = lax.all_to_all(spread, front, 0, 0, tiled=True).reshape(HALF * SPREAD, 128)
     other = lax.ppermute(gathered, "core", swap)
 
     return pl.pallas_call(
         solve_kernel,
         out_shape=jax.ShapeDtypeStruct((LEVELS, ROWS, SHOTS), F32),
-        in_specs=[SMEM] * 2 + [VMEM] * 6,
+        in_specs=[VMEM] * 7,
         out_specs=HBM,
         scratch_shapes=[
             pltpu.VMEM((LEVELS, ROWS, SHOTS), F32),
             pltpu.SemaphoreType.DMA((LEVELS,)),
         ],
         compiler_params=params(SOLVE),
-    )(core, rank_sizes, gathered, other, own, forward, up, down)
+    )(rank_sizes.reshape(1, -1), gathered, other, own, forward, up, down)
 
 
 def solution(mesh):

time: 112 us -> 108 us (0.964); the launches traced: 110 us -> 107 us
  blocking collectives: 44.5 us -> 69 us
  starting transfers between devices: 33.6 us -> 20.3 us
  waiting for transfers between devices: 15 us -> 3.36 us
  Pallas kernels: 15.5 us -> 12.8 us
    all_to_all x1 -> x2, blocking collectives: 15.4 us -> 40.4 us  [the longest x1 24 us: per_device(): cross = lax.all_to_all(cross, ('zh', 'zl'), 0, 0, tiled=True)]
    all_to_all x1 -> x0, waiting for transfers between devices: 12.4 us -> none  [per_device(): lax.all_to_all(jnp.broadcast_to(reduced, (16, SENT, 128)), ('zh', 'zl'),...]
    all_to_all x1 -> x0, starting transfers between devices: 12.2 us -> none  [per_device(): lax.all_to_all(jnp.broadcast_to(reduced, (16, SENT, 128)), ('zh', 'zl'),...]
    pallas_call x1, Pallas kernels: 2.48 us -> 1.01 us  [per_device(): pl.pallas_call(bottom_kernel, out_shape=(jax.ShapeDtypeStruct((ROWS, SHOT...]
    unnamed x14 -> x16, local copies, waits for them, and re-layouts: 0.04 us -> 1.19 us
  transfers between devices with their start and end apart: 4 -> 3, of which waited for: 3 -> 2; matrix products, arithmetic and copies ran while one was open for 0% -> 0% of each run, Pallas kernels for 8% -> 6%
where the time goes in v2:
time: 108 us; the launch traced here: 107 us
  blocking collectives  69 us (64%)
  starting transfers between devices  20.3 us (19%)
  Pallas kernels  12.8 us (12%)
  waiting for transfers between devices  3.36 us (3%)
  local copies, waits for them, and re-layouts  1.19 us (1%)
    all_to_all x1, blocking collectives, per_device(): cross = lax.all_to_all(cross, ('zh', 'zl'), 0, 0, tiled=True)  24 us
    all_to_all x1, blocking collectives, per_device(): lax.all_to_all(message.reshape(FRONT, MESSAGE, 128), front, 0, 0, tiled=T...  17.4 us
    all_to_all x1, blocking collectives, per_device(): lax.all_to_all(spread, front, 0, 0, tiled=True).reshape(HALF * SPREAD, 128)  16.4 us
    all_to_all x1, blocking collectives, per_device(): pieces = lax.all_to_all(summed, ('zl', 'core'), 0, 0, tiled=True)  11.1 us
    all_to_all x1, starting transfers between devices, per_device(): lax.all_to_all(packed.reshape(FRONT, SLOTS, SHOTS + 128), front, 0, 0, ti...  7.6 us
    ppermute x1, starting transfers between devices, per_device(): other = lax.ppermute(gathered, 'core', swap)  6.83 us
    ppermute x1, starting transfers between devices, per_device(): other = lax.ppermute(send, 'core', swap)  5.83 us
    pallas_call x1, Pallas kernels, per_device(): pl.pallas_call(local_kernel, out_shape=(jax.ShapeDtypeStruct((LEVELS - 1,...  5.81 us
  transfers between devices with their start and end apart: 3, of which 2 were waited for; matrix products, arithmetic and copies ran while one was open for 0% of the time, Pallas kernels for 6%

profile of v2, /device:TPU:1, one launch (start us, length us, event | category | flops | bytes accessed | tf_op | source)
XLA Modules:
  0.0 107.4 jit_solution(742910024078082135)
XLA Ops:
  0.7 1.9 %shard_map.91 = f32[128,384]{1,0:T(8,128)} custom-call(s32[1]{0:T(128)S(6)} %copy.10.live_ref, f32[64,256]{1,0:T(8,128)} %resid_hbm.1, s32[1,64]{1,0:T(1,128)} %bitcast.13, s32[1,64]{1,0:T(1,128)} %bitcast.14), custom_call_target="tpu_custom_call" | custom-call | tf_op jit(solution)/shard_map/pallas_call | solution.py:319
  2.6 7.6 %all-to-all-start = ((f32[16,8,384]{2,1,0:T(8,128)}), f32[16,8,384]{2,1,0:T(8,128)S(1)}, u32[]{:S(2)}, u32[]{:S(2)}) async-start(f32[16,8,384]{2,1,0:T(8,128)} %bitcast.12), calls=%async_computation | async-start | bytes 393216 | tf_op jit(solution)/shard_map/all_to_all | solution.py:333
  10.2 0.0 copy-start.1
  10.2 0.0 copy-start.6
  10.2 5.8 %shard_map.92 = (f32[3,384,256]{2,1,0:T(8,128)}, bf16[3,2,384,128]{3,2,1,0:T(8,128)(2,1)}, bf16[3,2,384,128]{3,2,1,0:T(8,128)(2,1)}, f32[1152,128]{1,0:T(8,128)}, f32[1152,128]{1,0:T(8,128)}) custom-call(bf16[4,384,256]{2,1,0:T(8,128)(2,1)} %rhs_ref.1, bf16[4,384,384]{2,1,0:T(8,128)(2,1)} %dinv_ref.1, bf16[3,384,128]{2,1,0:T(8,128)(2,1)} %u_hbm.1, ...), custom_call_target="tpu_custom_call" | custom-call | flops 2000000000 | bytes 8000000 | tf_op jit(solution)/shard_map/pallas_call | solution.py:339
  16.0 1.1 %all-to-all-done = f32[16,8,384]{2,1,0:T(8,128)S(1)} async-done(((f32[16,8,384]{2,1,0:T(8,128)}), f32[16,8,384]{2,1,0:T(8,128)S(1)}, u32[]{:S(2)}, u32[]{:S(2)}) %all-to-all-start) | async-done | bytes 196640 | tf_op jit(solution)/shard_map/all_to_all | solution.py:333
  17.1 5.8 %collective-permute-start = (f32[1152,128]{1,0:T(8,128)}, f32[1152,128]{1,0:T(8,128)S(1)}, u32[]{:S(2)}, u32[]{:S(2)}) collective-permute-start(f32[1152,128]{1,0:T(8,128)} %get-tuple-element.24), channel_id=1, source_target_pairs={{0,16},{16,0},{1,17},{17,1},{2,18},{18,2},{3,19},{19,3},{4,20},{20... | collective-permute-start | bytes 1769480 | tf_op jit(solution)/shard_map/ppermute | solution.py:369
  23.0 0.0 copy-done.1
  23.0 0.0 copy-start.2
  23.0 1.1 %copy-done.2 = bf16[4,384,256]{2,1,0:T(8,128)(2,1)S(1)} copy-done((bf16[4,384,256]{2,1,0:T(8,128)(2,1)S(1)}, bf16[4,384,256]{2,1,0:T(8,128)(2,1)}, u32[]{:S(2)}) %copy-start.2) | copy-done | bytes 786456
  24.1 1.0 shard_map.93
  25.1 0.0 collective-permute-done.other_ref
  25.1 0.0 copy-done.5
  25.2 0.1 shard_map.94
  25.3 17.4 %all_to_all.25.pieces_ref = f32[16,88,128]{2,1,0:T(8,128)S(1)} all-to-all(f32[16,88,128]{2,1,0:T(8,128)S(1)} %bitcast.9), channel_id=1, replica_groups=mesh['zh'=4,'zl'=4,'core'=2,'x'=4,'y'=4] {'x','y'}, dimensions={0} | all-to-all | bytes 1441792 | tf_op jit(solution)/shard_map/all_to_all | solution.py:388
  42.7 11.1 %all_to_all.26.pieces_ref = f32[8,32,128]{2,1,0:T(8,128)S(1)} all-to-all(f32[8,32,128]{2,1,0:T(8,128)S(1)} %shard_map.95), channel_id=1, replica_groups=mesh['zh'=4,'zl'=4,'core'=2,'x'=4,'y'=4] {'zl','core'}, dimensions={0} | all-to-all | bytes 262144 | tf_op jit(solution)/shard_map/all_to_all | solution.py:396
  53.9 24.0 %all_to_all.27.cross_ref = f32[16,16,128]{2,1,0:T(8,128)S(1)} all-to-all(f32[16,16,128]{2,1,0:T(8,128)S(1)} %get-tuple-element.25), channel_id=1, replica_groups=mesh['zh'=4,'zl'=4,'core'=2,'x'=4,'y'=4] {'zh','zl'}, dimensions={0} | all-to-all | bytes 262144 | tf_op jit(solution)/shard_map/all_to_all | solution.py:407
  77.9 0.1 shard_map.97
  78.0 0.0 copy-start
  78.0 0.0 copy-start.7
  78.0 16.4 %all_to_all.28 = f32[16,128,128]{2,1,0:T(8,128)S(1)} all-to-all(f32[16,128,128]{2,1,0:T(8,128)S(1)} %shard_map.97), channel_id=1, replica_groups=mesh['zh'=4,'zl'=4,'core'=2,'x'=4,'y'=4] {'x','y'}, dimensions={0} | all-to-all | bytes 2097152 | tf_op jit(solution)/shard_map/all_to_all | solution.py:415
  94.4 6.8 %collective-permute-start.1 = (f32[2048,128]{1,0:T(8,128)S(1)}, f32[2048,128]{1,0:T(8,128)S(1)}, u32[]{:S(2)}, u32[]{:S(2)}) collective-permute-start(f32[2048,128]{1,0:T(8,128)S(1)} %bitcast.7), channel_id=1, source_target_pairs={{0,16},{16,0},{1,17},{17,1},{2,18},{18,2},{3,19},{19,3},{4,20},{20... | collective-permute-start | bytes 3145736 | tf_op jit(solution)/shard_map/ppermute | solution.py:416
  101.3 2.3 %collective-permute-done.1.other_ref = f32[2048,128]{1,0:T(8,128)S(1)} collective-permute-done((f32[2048,128]{1,0:T(8,128)S(1)}, f32[2048,128]{1,0:T(8,128)S(1)}, u32[]{:S(2)}, u32[]{:S(2)}) %collective-permute-start.1) | collective-permute-done | bytes 1048608 | tf_op jit(solution)/shard_map/ppermute | solution.py:416
  103.6 3.9 %shard_map.98 = f32[4,384,256]{2,1,0:T(8,128)} custom-call(s32[1,3]{1,0:T(1,128)S(1)} %bitcast.11, f32[2048,128]{1,0:T(8,128)S(1)} %bitcast.8, f32[2048,128]{1,0:T(8,128)S(1)} %collective-permute-done.1.other_ref, f32[3,384,256]{2,1,0:T(8,128)S(1)} %copy-done, f32[384,256]{1,0:T(8,128)S(1)} %get-tuple-element.28.forward_ref, ...), custom_call_target="tpu_custom_call" | custom-call | tf_op jit(solution)/shard_map/pallas_call | solution.py:418
  (10 shorter events, 0.1 us)
Async XLA Ops:
  2.6 14.5 %all-to-all-start = ((f32[16,8,384]{2,1,0:T(8,128)}), f32[16,8,384]{2,1,0:T(8,128)S(1)}, u32[]{:S(2)}, u32[]{:S(2)}) async-start(f32[16,8,384]{2,1,0:T(8,128)} %bitcast.12), calls=%async_computation | async-start | bytes 393216 | tf_op jit(solution)/shard_map/all_to_all | solution.py:333
  10.2 12.8 %copy-start.1 = (bf16[4,384,384]{2,1,0:T(8,128)(2,1)S(1)}, bf16[4,384,384]{2,1,0:T(8,128)(2,1)}, u32[]{:S(2)}) copy-start(bf16[4,384,384]{2,1,0:T(8,128)(2,1)} %dinv_ref.1) | copy-start | bytes 3538948
  10.2 12.8 %copy-start.6 = (bf16[3,384,128]{2,1,0:T(8,128)(2,1)S(1)}, bf16[3,384,128]{2,1,0:T(8,128)(2,1)}, u32[]{:S(2)}) copy-start(bf16[3,384,128]{2,1,0:T(8,128)(2,1)} %v_ref.1) | copy-start | bytes 884740
  17.1 8.0 %collective-permute-start = (f32[1152,128]{1,0:T(8,128)}, f32[1152,128]{1,0:T(8,128)S(1)}, u32[]{:S(2)}, u32[]{:S(2)}) collective-permute-start(f32[1152,128]{1,0:T(8,128)} %get-tuple-element.24), channel_id=1, source_target_pairs={{0,16},{16,0},{1,17},{17,1},{2,18},{18,2},{3,19},{19,3},{4,20},{20... | collective-permute-start | bytes 1769480 | tf_op jit(solution)/shard_map/ppermute | solution.py:369
  23.0 1.1 %copy-start.2 = (bf16[4,384,256]{2,1,0:T(8,128)(2,1)S(1)}, bf16[4,384,256]{2,1,0:T(8,128)(2,1)}, u32[]{:S(2)}) copy-start(bf16[4,384,256]{2,1,0:T(8,128)(2,1)} %rhs_ref.1) | copy-start | bytes 2359300
  24.1 1.1 copy-start.5
  77.9 25.6 %copy-start.4 = (bf16[3,2,384,128]{3,2,1,0:T(8,128)(2,1)S(1)}, bf16[3,2,384,128]{3,2,1,0:T(8,128)(2,1)}, u32[]{:S(2)}) copy-start(bf16[3,2,384,128]{3,2,1,0:T(8,128)(2,1)} %get-tuple-element.30.down_ref) | copy-start | bytes 1769476
  78.0 25.5 %copy-start = (f32[3,384,256]{2,1,0:T(8,128)S(1)}, f32[3,384,256]{2,1,0:T(8,128)}, u32[]{:S(2)}) copy-start(f32[3,384,256]{2,1,0:T(8,128)} %get-tuple-element.27.own_ref) | copy-start | bytes 3538948
  78.0 25.5 %copy-start.3 = (bf16[3,2,384,128]{3,2,1,0:T(8,128)(2,1)S(1)}, bf16[3,2,384,128]{3,2,1,0:T(8,128)(2,1)}, u32[]{:S(2)}) copy-start(bf16[3,2,384,128]{3,2,1,0:T(8,128)(2,1)} %get-tuple-element.29.up_ref) | copy-start | bytes 1769476
  78.0 25.5 %copy-start.7 = (s32[3]{0:T(128)S(1)}, s32[3]{0:T(128)}, u32[]{:S(2)}) copy-start(s32[3]{0:T(128)} %param.13) | copy-start | bytes 40
  94.4 9.1 %collective-permute-start.1 = (f32[2048,128]{1,0:T(8,128)S(1)}, f32[2048,128]{1,0:T(8,128)S(1)}, u32[]{:S(2)}, u32[]{:S(2)}) collective-permute-start(f32[2048,128]{1,0:T(8,128)S(1)} %bitcast.7), channel_id=1, source_target_pairs={{0,16},{16,0},{1,17},{17,1},{2,18},{18,2},{3,19},{19,3},{4,20},{20... | collective-permute-start | bytes 3145736 | tf_op jit(solution)/shard_map/ppermute | solution.py:416

commit v3 on v2

--- a/solution.py
+++ b/solution.py
@@ -34,7 +34,8 @@
 
 
 SOLVE = 16
-WHOLE = 62
+LOCAL = 54
+WHOLE = 54
 
 
 def params(mebibytes):
@@ -100,13 +101,12 @@
     front = column(front_ref, recv)
     copies[1].wait()
     rows = jnp.where(live, column(row_ref, recv) + 1, 0)
-    onehot = front == lax.broadcasted_iota(jnp.int32, (recv, FRONT), 1)
-    earlier = lax.broadcasted_iota(jnp.int32, (recv, recv), 0) > lax.broadcasted_iota(
-        jnp.int32, (recv, recv), 1
+    same = (front == front_ref[...]) & (
+        lax.broadcasted_iota(jnp.int32, (recv, recv), 1)
+        < lax.broadcasted_iota(jnp.int32, (recv, recv), 0)
     )
-    before = mm(earlier.astype(F32).astype(BF16), onehot.astype(F32).astype(BF16))
-    position = jnp.sum(jnp.where(onehot, before, 0.0), axis=1, keepdims=True)
-    slot = front * SLOTS + position.astype(jnp.int32)
+    position = jnp.sum(same.astype(jnp.int32), axis=1, keepdims=True)
+    slot = front * SLOTS + position
     place = slot == lax.broadcasted_iota(jnp.int32, (recv, FRONT * SLOTS), 1)
     place = place.astype(F32).astype(BF16)
     copies[2].wait()
@@ -118,31 +118,27 @@
 
 
 def local_kernel(
-    rhs_hbm, dinv_hbm, u_hbm, v_hbm,
-    own_hbm, up_hbm, down_hbm, mine_ref, send_ref,
-    rhs_ref, dinv_ref, u_ref, v_ref, own_ref, up_ref, down_ref, wide_ref, narrow_ref,
-    in_sems, out_sems,
+    rhs_hbm, dinv_hbm, u_hbm, v_hbm, mine_ref, send_ref,
+    rhs_ref, dinv_ref, u_ref, v_ref, wide_ref, narrow_ref, sems,
 ):
     core = lax.axis_index("core")
     loads = []
-    for level in range(LEVELS):
-        pairs = [(dinv_hbm, dinv_ref)]
-        if level < LEVELS - 1:
-            pairs += [(rhs_hbm, rhs_ref), (u_hbm, u_ref), (v_hbm, v_ref)]
+    for level in range(LEVELS - 1):
+        pairs = [
+            (dinv_hbm.at[level], dinv_ref.at[level]),
+            (rhs_hbm.at[level], rhs_ref.at[level]),
+            (u_hbm.at[level], u_ref.at[level]),
+        ]
+        if level > 0:
+            pairs.append((v_hbm.at[level - 1], v_ref.at[level - 1]))
         loads.append(
             [
-                pltpu.make_async_copy(source.at[level], target.at[level], in_sems.at[level, index])
+                pltpu.make_async_copy(source, target, sems.at[level, index])
                 for index, (source, target) in enumerate(pairs)
             ]
         )
         for copy in loads[-1]:
             copy.start()
-    stores = []
-
-    def keep(source, target):
-        copy = pltpu.make_async_copy(source, target, out_sems.at[len(stores)])
-        copy.start()
-        stores.append(copy)
 
     def reduce(factor, pair):
         return mm_tn(factor, pair[0]) + mm_tn(factor, pair[1])
@@ -156,33 +152,32 @@
             mine_ref[rows, :] = scratch[pl.ds(core * HALF, HALF), lanes]
             send_ref[rows, :] = scratch[pl.ds((1 - core) * HALF, HALF), lanes]
 
-    mine_ref[...] = jnp.zeros_like(mine_ref)
-    send_ref[...] = jnp.zeros_like(send_ref)
-    for level in range(LEVELS):
+    save(PART - 1, jnp.zeros((RANK, 128), F32))
+    for level in range(LEVELS - 1):
         for copy in loads[level]:
             copy.wait()
         block = dinv_ref[level]
-        if level > 0:
-            down = split(mm(block, v_ref[level - 1]))
-            down_ref[level - 1, 0], down_ref[level - 1, 1] = down
-            keep(down_ref.at[level - 1], down_hbm.at[level - 1])
-        if level == LEVELS - 1:
-            continue
-        own = mm(block, rhs_ref[level])
-        own_ref[level] = own
-        keep(own_ref.at[level], own_hbm.at[level])
+        own = split(mm(block, rhs_ref[level]))
         up = split(mm(block, u_ref[level]))
-        up_ref[level, 0], up_ref[level, 1] = up
-        keep(up_ref.at[level], up_hbm.at[level])
-        own = split(own)
         save((S0, S1, S2)[level], reduce(u_ref[level], own))
         save((B0, B1, B2)[level], reduce(u_ref[level], up))
         if level > 0:
+            down = split(mm(block, v_ref[level - 1]))
             save((None, R0V, R1V)[level], reduce(v_ref[level - 1], own))
             save((None, A1, A2)[level], reduce(v_ref[level - 1], up))
             save((None, C1, C2)[level], reduce(u_ref[level], down))
-    for copy in stores:
-        copy.wait()
+
+
+def fields_kernel(rhs_ref, dinv_ref, u_ref, v_ref, own_ref, mix_ref):
+    for level in range(LEVELS):
+        block = dinv_ref[level]
+        if level < LEVELS - 1:
+            own_ref[level] = mm(block, rhs_ref[level])
+            for part, value in enumerate(split(mm(block, u_ref[level]))):
+                mix_ref[level, part, :, :RANK] = value
+        if level > 0:
+            for part, value in enumerate(split(mm(block, v_ref[level - 1]))):
+                mix_ref[level, part, :, RANK:] = value
 
 
 def bottom_kernel(got_ref, dinv_ref, v_ref, rhs_ref, forward_ref, coupled_ref):
@@ -263,52 +258,58 @@
 
 
 def solve_kernel(
-    rank_ref, mine_ref, other_ref, own_ref, forward_ref, up_ref, down_ref, out_hbm,
+    rank_ref, mine_ref, other_ref, own_ref, forward_ref, mix_ref, out_hbm,
     out_ref, out_sems,
 ):
-    stores = []
-
-    def finish(level, value):
-        out_ref[level] = value
-        copy = pltpu.make_async_copy(out_ref.at[level], out_hbm.at[level], out_sems.at[level])
-        copy.start()
-        stores.append(copy)
-
-    first = lax.axis_index("core") == 0
-
-    def block(at):
-        mine = mine_ref[pl.ds(at, HALF, stride=SPREAD), :]
-        other = other_ref[pl.ds(at, HALF, stride=SPREAD), :]
-        return jnp.concatenate(
-            [jnp.where(first, mine, other), jnp.where(first, other, mine)], axis=0
-        )
-
-    def wide(at):
-        return jnp.concatenate([block(at), block(at + 1)], axis=1)
-
-    def mask(coupling, value):
-        keep = lax.broadcasted_iota(jnp.int32, value.shape, 0) < rank_ref[:, coupling : coupling + 1]
-        return jnp.where(keep, value, 0.0)
-
-    def expand(pair_ref, index, value):
-        high, low = split(value)
-        left_high, left_low = pair_ref[index, 0], pair_ref[index, 1]
-        return mm(left_high, high) + (mm(left_high, low) + mm(left_low, high))
-
-    c2 = [mask(2, wide(G_R2V + 2 * node)) for node in range(4)]
-    t1 = [mm3(block(G_A2 + node), c2[node]) for node in range(4)]
-    c1 = [mask(1, wide(G_R1V + 2 * half) - (t1[2 * half] + t1[2 * half + 1])) for half in range(2)]
-    t0 = [mm3(block(G_A1 + half), c1[half]) for half in range(2)]
-    c0 = mask(0, wide(G_R0V) - (t0[0] + t0[1]))
-    d0 = mask(0, wide(G_S0) - mm3(block(G_B0), c0))
-    d1 = mask(1, wide(G_S1) - mm3(block(G_B1), c1[0]) - mm3(block(G_C1), d0))
-    d2 = mask(2, wide(G_S2) - mm3(block(G_B2), c2[0]) - mm3(block(G_C2), d1))
-    finish(0, own_ref[0] - expand(up_ref, 0, c0))
-    finish(1, own_ref[1] - expand(up_ref, 1, c1[0]) - expand(down_ref, 0, d0))
-    finish(2, own_ref[2] - expand(up_ref, 2, c2[0]) - expand(down_ref, 1, d1))
-    finish(3, forward_ref[...] - expand(down_ref, 2, d2))
-    for copy in stores:
-        copy.wait()
+    def solve(low_ref, high_ref):
+        stores = []
+
+        def finish(level, value):
+            out_ref[level] = value
+            copy = pltpu.make_async_copy(out_ref.at[level], out_hbm.at[level], out_sems.at[level])
+            copy.start()
+            stores.append(copy)
+
+        def block(at):
+            rows = pl.ds(at, HALF, stride=SPREAD)
+            return jnp.concatenate([low_ref[rows, :], high_ref[rows, :]], axis=0)
+
+        def wide(at):
+            return jnp.concatenate([block(at), block(at + 1)], axis=1)
+
+        def mask(coupling, value):
+            keep = lax.broadcasted_iota(jnp.int32, value.shape, 0) < rank_ref[:, coupling : coupling + 1]
+            return jnp.where(keep, value, 0.0)
+
+        def expand(level, lanes, *values):
+            high, low = split(jnp.concatenate(values, axis=0))
+            left_high, left_low = mix_ref[level, 0, :, lanes], mix_ref[level, 1, :, lanes]
+            return mm(left_high, high) + (mm(left_high, low) + mm(left_low, high))
+
+        def couple(blocks, values):
+            left = [block(at) for at in blocks]
+            return mm3(jnp.concatenate(left, axis=1), jnp.concatenate(values, axis=0))
+
+        c2 = [mask(2, wide(G_R2V + 2 * node)) for node in range(4)]
+        t1 = [
+            couple((G_A2 + 2 * half, G_A2 + 2 * half + 1), c2[2 * half : 2 * half + 2])
+            for half in range(2)
+        ]
+        c1 = [mask(1, wide(G_R1V + 2 * half) - t1[half]) for half in range(2)]
+        c0 = mask(0, wide(G_R0V) - couple((G_A1, G_A1 + 1), c1))
+        d0 = mask(0, wide(G_S0) - couple((G_B0,), (c0,)))
+        finish(0, own_ref[0] - expand(0, slice(0, RANK), c0))
+        d1 = mask(1, wide(G_S1) - couple((G_B1, G_C1), (c1[0], d0)))
+        finish(1, own_ref[1] - expand(1, slice(0, 2 * RANK), c1[0], d0))
+        d2 = mask(2, wide(G_S2) - couple((G_B2, G_C2), (c2[0], d1)))
+        finish(2, own_ref[2] - expand(2, slice(0, 2 * RANK), c2[0], d1))
+        finish(3, forward_ref[...] - expand(3, slice(RANK, 2 * RANK), d2))
+        for copy in stores:
+            copy.wait()
+
+    core = lax.axis_index("core")
+    pl.when(core == 0)(lambda: solve(mine_ref, other_ref))
+    pl.when(core == 1)(lambda: solve(other_ref, mine_ref))
 
 
 def per_device(rhs, dinv, u_factor, v_factor, rank_sizes, resid, dest_front, dest_row, live_count):
@@ -334,38 +335,26 @@
         packed.reshape(FRONT, SLOTS, SHOTS + 128), front, 0, 0, tiled=True
     ).reshape(FRONT * SLOTS, SHOTS + 128)
 
-    pair = jax.ShapeDtypeStruct((LEVELS - 1, 2, ROWS, RANK), BF16)
     early = jax.ShapeDtypeStruct((HALF * PART, 128), F32)
-    own, up, down, mine, send = pl.pallas_call(
+    mine, send = pl.pallas_call(
         local_kernel,
-        out_shape=(
-            jax.ShapeDtypeStruct((LEVELS - 1, ROWS, SHOTS), F32),
-            pair,
-            pair,
-            early,
-            early,
-        ),
+        out_shape=(early, early),
         in_specs=[HBM] * 4,
-        out_specs=(HBM,) * 3 + (VMEM,) * 2,
+        out_specs=(VMEM, VMEM),
         scratch_shapes=[
-            pltpu.VMEM(rhs.shape, BF16),
-            pltpu.VMEM(dinv.shape, BF16),
-            pltpu.VMEM(u_factor.shape, BF16),
-            pltpu.VMEM(v_factor.shape, BF16),
-            pltpu.VMEM((LEVELS - 1, ROWS, SHOTS), F32),
-            pltpu.VMEM(pair.shape, BF16),
-            pltpu.VMEM(pair.shape, BF16),
+            pltpu.VMEM((LEVELS - 1, ROWS, SHOTS), BF16),
+            pltpu.VMEM((LEVELS - 1, ROWS, ROWS), BF16),
+            pltpu.VMEM((LEVELS - 1, ROWS, RANK), BF16),
+            pltpu.VMEM((LEVELS - 2, ROWS, RANK), BF16),
             pltpu.VMEM((RANK, SHOTS), F32),
             pltpu.VMEM((RANK, RANK), F32),
-            pltpu.SemaphoreType.DMA((LEVELS, 4)),
-            pltpu.SemaphoreType.DMA((9,)),
+            pltpu.SemaphoreType.DMA((LEVELS - 1, 4)),
         ],
-        compiler_params=params(WHOLE),
+        compiler_params=params(LOCAL),
         cost_estimate=pl.CostEstimate(
-            flops=2_000_000_000, bytes_accessed=8_000_000, transcendentals=0
+            flops=20_000_000_000, bytes_accessed=8_000_000, transcendentals=0
         ),
     )(rhs, dinv_after, u_factor, v_factor)
-    got, send = lax.optimization_barrier((got, send))
     other = lax.ppermute(send, "core", swap)
 
     forward, coupled = pl.pallas_call(
@@ -377,6 +366,9 @@
         in_specs=[VMEM] * 4,
         out_specs=(VMEM, VMEM),
         compiler_params=params(8),
+        cost_estimate=pl.CostEstimate(
+            flops=20_000_000_000, bytes_accessed=4_000_000, transcendentals=0
+        ),
     )(got, dinv, v_factor, rhs)
     message = pl.pallas_call(
         message_kernel,
@@ -385,6 +377,21 @@
         out_specs=VMEM,
         compiler_params=params(4),
     )(coupled, mine, other)
+
+    message, dinv_late = lax.optimization_barrier((message, dinv))
+    own, mix = pl.pallas_call(
+        fields_kernel,
+        out_shape=(
+            jax.ShapeDtypeStruct((LEVELS - 1, ROWS, SHOTS), F32),
+            jax.ShapeDtypeStruct((LEVELS, 2, ROWS, 2 * RANK), BF16),
+        ),
+        in_specs=[VMEM] * 4,
+        out_specs=(VMEM,) * 2,
+        compiler_params=params(8),
+        cost_estimate=pl.CostEstimate(
+            flops=1_200_000_000, bytes_accessed=5_000_000, transcendentals=0
+        ),
+    )(rhs, dinv_late, u_factor, v_factor)
     pieces = lax.all_to_all(message.reshape(FRONT, MESSAGE, 128), front, 0, 0, tiled=True)
     summed = pl.pallas_call(
         total_kernel,
@@ -418,14 +425,14 @@
     return pl.pallas_call(
         solve_kernel,
         out_shape=jax.ShapeDtypeStruct((LEVELS, ROWS, SHOTS), F32),
-        in_specs=[VMEM] * 7,
+        in_specs=[VMEM] * 6,
         out_specs=HBM,
         scratch_shapes=[
             pltpu.VMEM((LEVELS, ROWS, SHOTS), F32),
             pltpu.SemaphoreType.DMA((LEVELS,)),
         ],
         compiler_params=params(SOLVE),
-    )(rank_sizes.reshape(1, -1), gathered, other, own, forward, up, down)
+    )(rank_sizes.reshape(1, -1), gathered, other, own, forward, mix)
 
 
 def solution(mesh):

time: 108 us -> 106 us (0.981)
  blocking collectives: 69 us -> 71 us
  waiting for transfers between devices: 3.36 us -> 2.06 us
  local copies, waits for them, and re-layouts: 1.19 us -> 0.03 us
    all_to_all x1, blocking collectives: 17.4 us -> 19.2 us  [per_device(): lax.all_to_all(message.reshape(FRONT, MESSAGE, 128), front, 0, 0, tiled=T...]
    unnamed x16 -> x12, local copies, waits for them, and re-layouts: 1.19 us -> 0.03 us
    ppermute x1, starting transfers between devices: 5.83 us -> 4.71 us  [per_device(): other = lax.ppermute(send, 'core', swap)]
    all_to_all x1, waiting for transfers between devices: 1.09 us -> 0.01 us  [per_device(): lax.all_to_all(packed.reshape(FRONT, SLOTS, SHOTS + 128), front, 0, 0, ti...]
    pallas_call x1 -> x2, Pallas kernels: 5.81 us -> 5.73 us  [the longest x1 4.8 us: per_device(): pl.pallas_call(local_kernel, out_shape=(early, early), in_specs=[HBM] * 4...]
where the time goes in v3:
time: 106 us; the launch traced here: 105 us
  blocking collectives  71 us (67%)
  starting transfers between devices  19.3 us (18%)
  Pallas kernels  12 us (11%)
  waiting for transfers between devices  2.06 us (2%)
    all_to_all x1, blocking collectives, per_device(): cross = lax.all_to_all(cross, ('zh', 'zl'), 0, 0, tiled=True)  24 us
    all_to_all x1, blocking collectives, per_device(): lax.all_to_all(message.reshape(FRONT, MESSAGE, 128), front, 0, 0, tiled=T...  19.2 us
    all_to_all x1, blocking collectives, per_device(): lax.all_to_all(spread, front, 0, 0, tiled=True).reshape(HALF * SPREAD, 128)  16.3 us
    all_to_all x1, blocking collectives, per_device(): pieces = lax.all_to_all(summed, ('zl', 'core'), 0, 0, tiled=True)  11.6 us
    all_to_all x1, starting transfers between devices, per_device(): lax.all_to_all(packed.reshape(FRONT, SLOTS, SHOTS + 128), front, 0, 0, ti...  7.61 us
    ppermute x1, starting transfers between devices, per_device(): other = lax.ppermute(gathered, 'core', swap)  6.96 us
    pallas_call x1, Pallas kernels, per_device(): pl.pallas_call(local_kernel, out_shape=(early, early), in_specs=[HBM] * 4...  4.8 us
    ppermute x1, starting transfers between devices, per_device(): other = lax.ppermute(send, 'core', swap)  4.71 us
  transfers between devices with their start and end apart: 3, of which 2 were waited for; matrix products, arithmetic and copies ran while one was open for 0% of the time, Pallas kernels for 6%

profile of v3, /device:TPU:1, one launch (start us, length us, event | category | flops | bytes accessed | tf_op | source)
XLA Modules:
  0.0 105.2 jit_solution(3916247571922715594)
XLA Ops:
  0.7 1.8 %shard_map.91 = f32[128,384]{1,0:T(8,128)} custom-call(s32[1]{0:T(128)S(6)} %copy.10.live_ref, f32[64,256]{1,0:T(8,128)} %resid_hbm.1, s32[1,64]{1,0:T(1,128)} %bitcast.13, s32[1,64]{1,0:T(1,128)} %bitcast.14), custom_call_target="tpu_custom_call" | custom-call | tf_op jit(solution)/shard_map/pallas_call | solution.py:320
  2.5 7.6 %all-to-all-start = ((f32[16,8,384]{2,1,0:T(8,128)}), f32[16,8,384]{2,1,0:T(8,128)S(1)}, u32[]{:S(2)}, u32[]{:S(2)}) async-start(f32[16,8,384]{2,1,0:T(8,128)} %bitcast.12), calls=%async_computation | async-start | bytes 393216 | tf_op jit(solution)/shard_map/all_to_all | solution.py:334
  10.1 0.0 copy-start.2
  10.1 0.0 copy-start.3
  10.1 0.0 copy-start.4
  10.1 4.8 %shard_map.93 = (f32[1152,128]{1,0:T(8,128)}, f32[1152,128]{1,0:T(8,128)}) custom-call(bf16[4,384,256]{2,1,0:T(8,128)(2,1)} %rhs_ref.3, bf16[4,384,384]{2,1,0:T(8,128)(2,1)} %dinv_ref.2, bf16[3,384,128]{2,1,0:T(8,128)(2,1)} %u_ref.1, bf16[3,384,128]{2,1,0:T(8,128)(2,1)} %v_ref.3), custom_call_target="tpu_custom_call" | custom-call | flops 20000000000 | bytes 8000000 | tf_op jit(solution)/shard_map/pallas_call | solution.py:339
  14.9 4.7 %collective-permute-start = (f32[1152,128]{1,0:T(8,128)}, f32[1152,128]{1,0:T(8,128)S(1)}, u32[]{:S(2)}, u32[]{:S(2)}) collective-permute-start(f32[1152,128]{1,0:T(8,128)} %get-tuple-element.21), channel_id=1, source_target_pairs={{0,16},{16,0},{1,17},{17,1},{2,18},{18,2},{3,19},{19,3},{4,20},{20... | collective-permute-start | bytes 1769480 | tf_op jit(solution)/shard_map/ppermute | solution.py:358
  19.7 0.0 all-to-all-done
  19.7 0.0 copy-done.2
  19.7 0.0 copy-start
  19.7 1.0 shard_map.92
  20.7 0.7 collective-permute-done.other_ref
  21.5 0.0 copy-done
  21.5 0.1 shard_map.94
  21.6 19.2 %all_to_all.25.pieces_ref = f32[16,88,128]{2,1,0:T(8,128)S(1)} all-to-all(f32[16,88,128]{2,1,0:T(8,128)S(1)} %bitcast.9), channel_id=1, replica_groups=mesh['zh'=4,'zl'=4,'core'=2,'x'=4,'y'=4] {'x','y'}, dimensions={0} | all-to-all | bytes 1441792 | tf_op jit(solution)/shard_map/all_to_all | solution.py:395
  40.8 11.6 %all_to_all.26.pieces_ref = f32[8,32,128]{2,1,0:T(8,128)S(1)} all-to-all(f32[8,32,128]{2,1,0:T(8,128)S(1)} %shard_map.95), channel_id=1, replica_groups=mesh['zh'=4,'zl'=4,'core'=2,'x'=4,'y'=4] {'zl','core'}, dimensions={0} | all-to-all | bytes 262144 | tf_op jit(solution)/shard_map/all_to_all | solution.py:403
  52.4 24.0 %all_to_all.27.cross_ref = f32[16,16,128]{2,1,0:T(8,128)S(1)} all-to-all(f32[16,16,128]{2,1,0:T(8,128)S(1)} %get-tuple-element.23), channel_id=1, replica_groups=mesh['zh'=4,'zl'=4,'core'=2,'x'=4,'y'=4] {'zh','zl'}, dimensions={0} | all-to-all | bytes 262144 | tf_op jit(solution)/shard_map/all_to_all | solution.py:414
  76.4 0.1 shard_map.97
  76.5 16.3 %all_to_all.28 = f32[16,128,128]{2,1,0:T(8,128)S(1)} all-to-all(f32[16,128,128]{2,1,0:T(8,128)S(1)} %shard_map.97), channel_id=1, replica_groups=mesh['zh'=4,'zl'=4,'core'=2,'x'=4,'y'=4] {'x','y'}, dimensions={0} | all-to-all | bytes 2097152 | tf_op jit(solution)/shard_map/all_to_all | solution.py:422
  92.8 7.0 %collective-permute-start.1 = (f32[2048,128]{1,0:T(8,128)S(1)}, f32[2048,128]{1,0:T(8,128)S(1)}, u32[]{:S(2)}, u32[]{:S(2)}) collective-permute-start(f32[2048,128]{1,0:T(8,128)S(1)} %bitcast.7), channel_id=1, source_target_pairs={{0,16},{16,0},{1,17},{17,1},{2,18},{18,2},{3,19},{19,3},{4,20},{20... | collective-permute-start | bytes 3145736 | tf_op jit(solution)/shard_map/ppermute | solution.py:423
  99.7 0.0 copy-done.5
  99.7 0.9 shard_map.98
  100.7 1.3 %collective-permute-done.1.other_ref = f32[2048,128]{1,0:T(8,128)S(1)} collective-permute-done((f32[2048,128]{1,0:T(8,128)S(1)}, f32[2048,128]{1,0:T(8,128)S(1)}, u32[]{:S(2)}, u32[]{:S(2)}) %collective-permute-start.1) | collective-permute-done | bytes 1048608 | tf_op jit(solution)/shard_map/ppermute | solution.py:423
  102.0 3.2 %shard_map.99 = f32[4,384,256]{2,1,0:T(8,128)} custom-call(s32[1,3]{1,0:T(1,128)S(1)} %bitcast.11, f32[2048,128]{1,0:T(8,128)S(1)} %bitcast.8, f32[2048,128]{1,0:T(8,128)S(1)} %collective-permute-done.1.other_ref, f32[3,384,256]{2,1,0:T(8,128)S(1)} %get-tuple-element.26.own_ref, f32[384,256]{1,0:T(8,128)S(1)} %get-tuple-element.27.forward_ref, ...), custom_call_target="tpu_custom_call" | custom-call | tf_op jit(solution)/shard_map/pallas_call | solution.py:425
  (7 shorter events, 0.1 us)
Async XLA Ops:
  2.5 17.2 %all-to-all-start = ((f32[16,8,384]{2,1,0:T(8,128)}), f32[16,8,384]{2,1,0:T(8,128)S(1)}, u32[]{:S(2)}, u32[]{:S(2)}) async-start(f32[16,8,384]{2,1,0:T(8,128)} %bitcast.12), calls=%async_computation | async-start | bytes 393216 | tf_op jit(solution)/shard_map/all_to_all | solution.py:334
  10.1 9.6 %copy-start.2 = (bf16[4,384,384]{2,1,0:T(8,128)(2,1)S(1)}, bf16[4,384,384]{2,1,0:T(8,128)(2,1)}, u32[]{:S(2)}) copy-start(bf16[4,384,384]{2,1,0:T(8,128)(2,1)} %dinv_ref.2) | copy-start | bytes 3538948
  10.1 9.6 %copy-start.3 = (bf16[4,384,256]{2,1,0:T(8,128)(2,1)S(1)}, bf16[4,384,256]{2,1,0:T(8,128)(2,1)}, u32[]{:S(2)}) copy-start(bf16[4,384,256]{2,1,0:T(8,128)(2,1)} %rhs_ref.3) | copy-start | bytes 2359300
  10.1 9.6 %copy-start.4 = (bf16[3,384,128]{2,1,0:T(8,128)(2,1)S(1)}, bf16[3,384,128]{2,1,0:T(8,128)(2,1)}, u32[]{:S(2)}) copy-start(bf16[3,384,128]{2,1,0:T(8,128)(2,1)} %v_ref.3) | copy-start | bytes 884740
  14.9 6.5 %collective-permute-start = (f32[1152,128]{1,0:T(8,128)}, f32[1152,128]{1,0:T(8,128)S(1)}, u32[]{:S(2)}, u32[]{:S(2)}) collective-permute-start(f32[1152,128]{1,0:T(8,128)} %get-tuple-element.21), channel_id=1, source_target_pairs={{0,16},{16,0},{1,17},{17,1},{2,18},{18,2},{3,19},{19,3},{4,20},{20... | collective-permute-start | bytes 1769480 | tf_op jit(solution)/shard_map/ppermute | solution.py:358
  19.7 1.8 %copy-start = (f32[1152,128]{1,0:T(8,128)S(1)}, f32[1152,128]{1,0:T(8,128)}, u32[]{:S(2)}) copy-start(f32[1152,128]{1,0:T(8,128)} %get-tuple-element.20.mine_ref) | copy-start | bytes 1769476
  76.4 23.3 %copy-start.5 = (bf16[3,384,128]{2,1,0:T(8,128)(2,1)S(1)}, bf16[3,384,128]{2,1,0:T(8,128)(2,1)}, u32[]{:S(2)}) copy-start(bf16[3,384,128]{2,1,0:T(8,128)(2,1)} %u_ref.1) | copy-start | bytes 884740
  92.8 9.2 %copy-start.1 = (s32[3]{0:T(128)S(1)}, s32[3]{0:T(128)}, u32[]{:S(2)}) copy-start(s32[3]{0:T(128)} %param.13) | copy-start | bytes 40
  92.8 9.2 %collective-permute-start.1 = (f32[2048,128]{1,0:T(8,128)S(1)}, f32[2048,128]{1,0:T(8,128)S(1)}, u32[]{:S(2)}, u32[]{:S(2)}) collective-permute-start(f32[2048,128]{1,0:T(8,128)S(1)} %bitcast.7), channel_id=1, source_target_pairs={{0,16},{16,0},{1,17},{17,1},{2,18},{18,2},{3,19},{19,3},{4,20},{20... | collective-permute-start | bytes 3145736 | tf_op jit(solution)/shard_map/ppermute | solution.py:423

commit v4 on v3

--- a/solution.py
+++ b/solution.py
@@ -43,7 +43,6 @@
 
 
 VMEM = pl.BlockSpec(memory_space=pltpu.VMEM)
-SMEM = pl.BlockSpec(memory_space=pltpu.SMEM)
 HBM = pl.BlockSpec(memory_space=pltpu.HBM)
 
 
@@ -77,44 +76,43 @@
     return mm(left_high, right_high) + (mm(left_high, right_low) + mm(left_low, right_high))
 
 
-def column(row_ref, count):
-    diagonal = lax.broadcasted_iota(jnp.int32, (count, count), 0) == lax.broadcasted_iota(
-        jnp.int32, (count, count), 1
-    )
-    return jnp.sum(jnp.where(diagonal, row_ref[...], 0), axis=1, keepdims=True)
-
-
 def pack_kernel(
-    live_ref, resid_hbm, front_hbm, row_hbm, out_ref, resid_ref, front_ref, row_ref, sems
+    live_hbm, resid_hbm, front_hbm, row_hbm, out_ref,
+    live_ref, resid_ref, front_ref, row_ref, sems,
 ):
     copies = [
         pltpu.make_async_copy(source, target, sems.at[index])
         for index, (source, target) in enumerate(
-            ((front_hbm, front_ref), (row_hbm, row_ref), (resid_hbm, resid_ref))
+            (
+                (front_hbm, front_ref),
+                (row_hbm, row_ref),
+                (resid_hbm, resid_ref),
+                (live_hbm, live_ref),
+            )
         )
     ]
     for copy in copies:
         copy.start()
     recv = resid_ref.shape[0]
-    live = lax.broadcasted_iota(jnp.int32, (recv, 1), 0) < live_ref[0]
+    sublane = lax.broadcasted_iota(jnp.int32, (recv, recv), 0)
+    lane = lax.broadcasted_iota(jnp.int32, (recv, recv), 1)
     copies[0].wait()
-    front = column(front_ref, recv)
+    front = front_ref[...]
+    column = jnp.sum(jnp.where(sublane == lane, front, 0), axis=1, keepdims=True)
+    earlier = (column == front) & (sublane < lane)
+    slot = front * SLOTS + jnp.sum(earlier.astype(jnp.int32), axis=0, keepdims=True)
+    copies[3].wait()
+    live = lane[:1] < live_ref[...]
+    place = live & (
+        lax.broadcasted_iota(jnp.int32, (FRONT * SLOTS, recv), 0) == slot
+    )
     copies[1].wait()
-    rows = jnp.where(live, column(row_ref, recv) + 1, 0)
-    same = (front == front_ref[...]) & (
-        lax.broadcasted_iota(jnp.int32, (recv, recv), 1)
-        < lax.broadcasted_iota(jnp.int32, (recv, recv), 0)
-    )
-    position = jnp.sum(same.astype(jnp.int32), axis=1, keepdims=True)
-    slot = front * SLOTS + position
-    place = slot == lax.broadcasted_iota(jnp.int32, (recv, FRONT * SLOTS), 1)
+    rows = jnp.sum(jnp.where(place, row_ref[...] + 1, 0), axis=1, keepdims=True)
+    out_ref[:, SHOTS:] = jnp.broadcast_to(rows.astype(F32), (FRONT * SLOTS, 128))
     place = place.astype(F32).astype(BF16)
     copies[2].wait()
-    high, mid, low = split3(jnp.where(live, resid_ref[...], 0.0))
-    coarse = jnp.broadcast_to((rows & ~15).astype(F32), (recv, 128)).astype(BF16)
-    fine = jnp.broadcast_to((rows & 15).astype(F32), (recv, 128)).astype(BF16)
-    out_ref[:, :SHOTS] = mm_tn(place, high) + (mm_tn(place, mid) + mm_tn(place, low))
-    out_ref[:, SHOTS:] = mm_tn(place, coarse) + mm_tn(place, fine)
+    high, mid, low = split3(resid_ref[...])
+    out_ref[:, :SHOTS] = mm(place, high) + (mm(place, mid) + mm(place, low))
 
 
 def local_kernel(
@@ -140,9 +138,6 @@
         for copy in loads[-1]:
             copy.start()
 
-    def reduce(factor, pair):
-        return mm_tn(factor, pair[0]) + mm_tn(factor, pair[1])
-
     def save(at, value):
         scratch = narrow_ref if value.shape[1] == 128 else wide_ref
         scratch[...] = value
@@ -157,15 +152,21 @@
         for copy in loads[level]:
             copy.wait()
         block = dinv_ref[level]
+        factor = u_ref[level]
+        narrow = factor
+        if level > 0:
+            narrow = jnp.concatenate([factor, v_ref[level - 1]], axis=1)
+            factor = narrow
         own = split(mm(block, rhs_ref[level]))
-        up = split(mm(block, u_ref[level]))
-        save((S0, S1, S2)[level], reduce(u_ref[level], own))
-        save((B0, B1, B2)[level], reduce(u_ref[level], up))
+        mix = split(mm(block, narrow))
+        own = mm_tn(factor, own[0]) + mm_tn(factor, own[1])
+        mix = mm_tn(factor, mix[0]) + mm_tn(factor, mix[1])
+        save((S0, S1, S2)[level], own[:RANK])
+        save((B0, B1, B2)[level], mix[:RANK, :RANK])
         if level > 0:
-            down = split(mm(block, v_ref[level - 1]))
-            save((None, R0V, R1V)[level], reduce(v_ref[level - 1], own))
-            save((None, A1, A2)[level], reduce(v_ref[level - 1], up))
-            save((None, C1, C2)[level], reduce(u_ref[level], down))
+            save((None, C1, C2)[level], mix[:RANK, RANK:])
+            save((None, R0V, R1V)[level], own[RANK:])
+            save((None, A1, A2)[level], mix[RANK:, :RANK])
 
 
 def fields_kernel(rhs_ref, dinv_ref, u_ref, v_ref, own_ref, mix_ref):
@@ -320,16 +321,17 @@
     packed = pl.pallas_call(
         pack_kernel,
         out_shape=jax.ShapeDtypeStruct((FRONT * SLOTS, SHOTS + 128), F32),
-        in_specs=[SMEM, HBM, HBM, HBM],
+        in_specs=[HBM] * 4,
         out_specs=VMEM,
         scratch_shapes=[
+            pltpu.VMEM((1, 1), jnp.int32),
             pltpu.VMEM(resid.shape, F32),
             pltpu.VMEM((1, resid.shape[0]), jnp.int32),
             pltpu.VMEM((1, resid.shape[0]), jnp.int32),
-            pltpu.SemaphoreType.DMA((3,)),
+            pltpu.SemaphoreType.DMA((4,)),
         ],
         compiler_params=params(WHOLE),
-    )(live_count, resid, dest_front.reshape(1, -1), dest_row.reshape(1, -1))
+    )(live_count.reshape(1, 1), resid, dest_front.reshape(1, -1), dest_row.reshape(1, -1))
     packed, dinv_after = lax.optimization_barrier((packed, dinv))
     got = lax.all_to_all(
         packed.reshape(FRONT, SLOTS, SHOTS + 128), front, 0, 0, tiled=True

time: 106 us -> 105 us (level)
  no operation moved by 1% of the time
where the time goes in v4:
time: 105 us
  blocking collectives  71 us (68%)
  starting transfers between devices  19.3 us (18%)
  Pallas kernels  11.8 us (11%)
  waiting for transfers between devices  2.06 us (2%)
    all_to_all x1, blocking collectives, per_device(): cross = lax.all_to_all(cross, ('zh', 'zl'), 0, 0, tiled=True)  24 us
    all_to_all x1, blocking collectives, per_device(): lax.all_to_all(message.reshape(FRONT, MESSAGE, 128), front, 0, 0, tiled=T...  19.2 us
    all_to_all x1, blocking collectives, per_device(): lax.all_to_all(spread, front, 0, 0, tiled=True).reshape(HALF * SPREAD, 128)  16.3 us
    all_to_all x1, blocking collectives, per_device(): pieces = lax.all_to_all(summed, ('zl', 'core'), 0, 0, tiled=True)  11.6 us
    all_to_all x1, starting transfers between devices, per_device(): lax.all_to_all(packed.reshape(FRONT, SLOTS, SHOTS + 128), front, 0, 0, ti...  7.6 us
    ppermute x1, starting transfers between devices, per_device(): other = lax.ppermute(gathered, 'core', swap)  6.96 us
    ppermute x1, starting transfers between devices, per_device(): other = lax.ppermute(send, 'core', swap)  4.72 us
    pallas_call x1, Pallas kernels, per_device(): pl.pallas_call(local_kernel, out_shape=(early, early), in_specs=[HBM] * 4...  4.57 us
  transfers between devices with their start and end apart: 3, of which 2 were waited for; matrix products, arithmetic and copies ran while one was open for 0% of the time, Pallas kernels for 6%

profile of v4, /device:TPU:1, one launch (start us, length us, event | category | flops | bytes accessed | tf_op | source)
XLA Modules:
  0.0 105.0 jit_solution(8342677710061420856)
XLA Ops:
  0.7 1.9 %shard_map.91 = f32[128,384]{1,0:T(8,128)} custom-call(s32[1,1]{1,0:T(1,128)} %bitcast.8.live_hbm, f32[64,256]{1,0:T(8,128)} %resid_hbm.1, s32[1,64]{1,0:T(1,128)} %bitcast.15, s32[1,64]{1,0:T(1,128)} %bitcast.16), custom_call_target="tpu_custom_call" | custom-call | tf_op jit(solution)/shard_map/pallas_call | solution.py:321
  2.5 7.6 %all-to-all-start = ((f32[16,8,384]{2,1,0:T(8,128)}), f32[16,8,384]{2,1,0:T(8,128)S(1)}, u32[]{:S(2)}, u32[]{:S(2)}) async-start(f32[16,8,384]{2,1,0:T(8,128)} %bitcast.14), calls=%async_computation | async-start | bytes 393216 | tf_op jit(solution)/shard_map/all_to_all | solution.py:336
  10.1 0.0 copy-start.2
  10.1 0.0 copy-start.3
  10.2 0.0 copy-start.4
  10.2 4.6 %shard_map.93 = (f32[1152,128]{1,0:T(8,128)}, f32[1152,128]{1,0:T(8,128)}) custom-call(bf16[4,384,256]{2,1,0:T(8,128)(2,1)} %rhs_ref.3, bf16[4,384,384]{2,1,0:T(8,128)(2,1)} %dinv_ref.2, bf16[3,384,128]{2,1,0:T(8,128)(2,1)} %u_ref.1, bf16[3,384,128]{2,1,0:T(8,128)(2,1)} %v_ref.3), custom_call_target="tpu_custom_call" | custom-call | flops 20000000000 | bytes 8000000 | tf_op jit(solution)/shard_map/pallas_call | solution.py:341
  14.7 4.7 %collective-permute-start = (f32[1152,128]{1,0:T(8,128)}, f32[1152,128]{1,0:T(8,128)S(1)}, u32[]{:S(2)}, u32[]{:S(2)}) collective-permute-start(f32[1152,128]{1,0:T(8,128)} %get-tuple-element.21), channel_id=1, source_target_pairs={{0,16},{16,0},{1,17},{17,1},{2,18},{18,2},{3,19},{19,3},{4,20},{20... | collective-permute-start | bytes 1769480 | tf_op jit(solution)/shard_map/ppermute | solution.py:360
  19.5 0.0 all-to-all-done
  19.5 0.0 copy-done.2
  19.5 0.0 copy-done.3
  19.5 0.0 copy-start
  19.5 1.0 shard_map.92
  20.6 0.7 collective-permute-done.other_ref
  21.3 0.1 shard_map.94
  21.4 19.2 %all_to_all.25.pieces_ref = f32[16,88,128]{2,1,0:T(8,128)S(1)} all-to-all(f32[16,88,128]{2,1,0:T(8,128)S(1)} %bitcast.11), channel_id=1, replica_groups=mesh['zh'=4,'zl'=4,'core'=2,'x'=4,'y'=4] {'x','y'}, dimensions={0} | all-to-all | bytes 1441792 | tf_op jit(solution)/shard_map/all_to_all | solution.py:397
  40.6 11.6 %all_to_all.26.pieces_ref = f32[8,32,128]{2,1,0:T(8,128)S(1)} all-to-all(f32[8,32,128]{2,1,0:T(8,128)S(1)} %shard_map.95), channel_id=1, replica_groups=mesh['zh'=4,'zl'=4,'core'=2,'x'=4,'y'=4] {'zl','core'}, dimensions={0} | all-to-all | bytes 262144 | tf_op jit(solution)/shard_map/all_to_all | solution.py:405
  52.2 24.0 %all_to_all.27.cross_ref = f32[16,16,128]{2,1,0:T(8,128)S(1)} all-to-all(f32[16,16,128]{2,1,0:T(8,128)S(1)} %get-tuple-element.23), channel_id=1, replica_groups=mesh['zh'=4,'zl'=4,'core'=2,'x'=4,'y'=4] {'zh','zl'}, dimensions={0} | all-to-all | bytes 262144 | tf_op jit(solution)/shard_map/all_to_all | solution.py:416
  76.2 0.1 shard_map.97
  76.3 16.3 %all_to_all.28 = f32[16,128,128]{2,1,0:T(8,128)S(1)} all-to-all(f32[16,128,128]{2,1,0:T(8,128)S(1)} %shard_map.97), channel_id=1, replica_groups=mesh['zh'=4,'zl'=4,'core'=2,'x'=4,'y'=4] {'x','y'}, dimensions={0} | all-to-all | bytes 2097152 | tf_op jit(solution)/shard_map/all_to_all | solution.py:424
  92.6 7.0 %collective-permute-start.1 = (f32[2048,128]{1,0:T(8,128)S(1)}, f32[2048,128]{1,0:T(8,128)S(1)}, u32[]{:S(2)}, u32[]{:S(2)}) collective-permute-start(f32[2048,128]{1,0:T(8,128)S(1)} %bitcast.9), channel_id=1, source_target_pairs={{0,16},{16,0},{1,17},{17,1},{2,18},{18,2},{3,19},{19,3},{4,20},{20... | collective-permute-start | bytes 3145736 | tf_op jit(solution)/shard_map/ppermute | solution.py:425
  99.6 0.9 shard_map.98
  100.5 1.3 %collective-permute-done.1.other_ref = f32[2048,128]{1,0:T(8,128)S(1)} collective-permute-done((f32[2048,128]{1,0:T(8,128)S(1)}, f32[2048,128]{1,0:T(8,128)S(1)}, u32[]{:S(2)}, u32[]{:S(2)}) %collective-permute-start.1) | collective-permute-done | bytes 1048608 | tf_op jit(solution)/shard_map/ppermute | solution.py:425
  101.8 0.0 copy-done.1
  101.8 3.2 %shard_map.99 = f32[4,384,256]{2,1,0:T(8,128)} custom-call(s32[1,3]{1,0:T(1,128)S(1)} %bitcast.13, f32[2048,128]{1,0:T(8,128)S(1)} %bitcast.10, f32[2048,128]{1,0:T(8,128)S(1)} %collective-permute-done.1.other_ref, f32[3,384,256]{2,1,0:T(8,128)S(1)} %get-tuple-element.26.own_ref, f32[384,256]{1,0:T(8,128)S(1)} %get-tuple-element.27.forward_ref, ...), custom_call_target="tpu_custom_call" | custom-call | tf_op jit(solution)/shard_map/pallas_call | solution.py:427
  (7 shorter events, 0.1 us)
Async XLA Ops:
  2.5 17.0 %all-to-all-start = ((f32[16,8,384]{2,1,0:T(8,128)}), f32[16,8,384]{2,1,0:T(8,128)S(1)}, u32[]{:S(2)}, u32[]{:S(2)}) async-start(f32[16,8,384]{2,1,0:T(8,128)} %bitcast.14), calls=%async_computation | async-start | bytes 393216 | tf_op jit(solution)/shard_map/all_to_all | solution.py:336
  10.1 9.4 %copy-start.2 = (bf16[4,384,384]{2,1,0:T(8,128)(2,1)S(1)}, bf16[4,384,384]{2,1,0:T(8,128)(2,1)}, u32[]{:S(2)}) copy-start(bf16[4,384,384]{2,1,0:T(8,128)(2,1)} %dinv_ref.2) | copy-start | bytes 3538948
  10.1 9.4 %copy-start.3 = (bf16[4,384,256]{2,1,0:T(8,128)(2,1)S(1)}, bf16[4,384,256]{2,1,0:T(8,128)(2,1)}, u32[]{:S(2)}) copy-start(bf16[4,384,256]{2,1,0:T(8,128)(2,1)} %rhs_ref.3) | copy-start | bytes 2359300
  10.2 9.4 %copy-start.4 = (bf16[3,384,128]{2,1,0:T(8,128)(2,1)S(1)}, bf16[3,384,128]{2,1,0:T(8,128)(2,1)}, u32[]{:S(2)}) copy-start(bf16[3,384,128]{2,1,0:T(8,128)(2,1)} %v_ref.3) | copy-start | bytes 884740
  14.7 6.5 %collective-permute-start = (f32[1152,128]{1,0:T(8,128)}, f32[1152,128]{1,0:T(8,128)S(1)}, u32[]{:S(2)}, u32[]{:S(2)}) collective-permute-start(f32[1152,128]{1,0:T(8,128)} %get-tuple-element.21), channel_id=1, source_target_pairs={{0,16},{16,0},{1,17},{17,1},{2,18},{18,2},{3,19},{19,3},{4,20},{20... | collective-permute-start | bytes 1769480 | tf_op jit(solution)/shard_map/ppermute | solution.py:360
  19.5 1.8 %copy-start = (f32[1152,128]{1,0:T(8,128)S(1)}, f32[1152,128]{1,0:T(8,128)}, u32[]{:S(2)}) copy-start(f32[1152,128]{1,0:T(8,128)} %get-tuple-element.20.mine_ref) | copy-start | bytes 1769476
  76.2 23.3 %copy-start.5 = (bf16[3,384,128]{2,1,0:T(8,128)(2,1)S(1)}, bf16[3,384,128]{2,1,0:T(8,128)(2,1)}, u32[]{:S(2)}) copy-start(bf16[3,384,128]{2,1,0:T(8,128)(2,1)} %u_ref.1) | copy-start | bytes 884740
  92.6 9.2 %copy-start.1 = (s32[3]{0:T(128)S(1)}, s32[3]{0:T(128)}, u32[]{:S(2)}) copy-start(s32[3]{0:T(128)} %param.13) | copy-start | bytes 40
  92.6 9.2 %collective-permute-start.1 = (f32[2048,128]{1,0:T(8,128)S(1)}, f32[2048,128]{1,0:T(8,128)S(1)}, u32[]{:S(2)}, u32[]{:S(2)}) collective-permute-start(f32[2048,128]{1,0:T(8,128)S(1)} %bitcast.9), channel_id=1, source_target_pairs={{0,16},{16,0},{1,17},{17,1},{2,18},{18,2},{3,19},{19,3},{4,20},{20... | collective-permute-start | bytes 3145736 | tf_op jit(solution)/shard_map/ppermute | solution.py:425

commit v5 on v4

--- a/solution.py
+++ b/solution.py
@@ -191,11 +191,16 @@
     high, mid, low = split3(got_ref[:, :SHOTS])
     block = dinv_ref[LEVELS - 1]
     chosen = mm_nt(block, select).astype(BF16)
-    forward = mm(block, rhs_ref[LEVELS - 1]) + (mm(chosen, high) + (mm(chosen, mid) + mm(chosen, low)))
+    twice = jnp.concatenate([chosen, chosen], axis=1)
+    forward = mm(block, rhs_ref[LEVELS - 1]) + (
+        mm(twice, jnp.concatenate([high, mid], axis=0)) + mm(chosen, low)
+    )
     forward_ref[...] = forward
     high, low = split(forward)
     factor = v_ref[LEVELS - 2]
-    coupled_ref[...] = mm_tn(factor, high) + mm_tn(factor, low)
+    coupled_ref[...] = mm_tn(
+        jnp.concatenate([factor, factor], axis=0), jnp.concatenate([high, low], axis=0)
+    )
 
 
 def message_kernel(coupled_ref, mine_ref, other_ref, out_ref):

time: 105 us -> 105 us (level)
  no operation moved by 1% of the time
where the time goes in v5:
time: 105 us
  blocking collectives  71 us (68%)
  starting transfers between devices  19.3 us (18%)
  Pallas kernels  11.7 us (11%)
  waiting for transfers between devices  2.17 us (2%)
    all_to_all x1, blocking collectives, per_device(): cross = lax.all_to_all(cross, ('zh', 'zl'), 0, 0, tiled=True)  24 us
    all_to_all x1, blocking collectives, per_device(): lax.all_to_all(message.reshape(FRONT, MESSAGE, 128), front, 0, 0, tiled=T...  19.2 us
    all_to_all x1, blocking collectives, per_device(): lax.all_to_all(spread, front, 0, 0, tiled=True).reshape(HALF * SPREAD, 128)  16.3 us
    all_to_all x1, blocking collectives, per_device(): pieces = lax.all_to_all(summed, ('zl', 'core'), 0, 0, tiled=True)  11.6 us
    all_to_all x1, starting transfers between devices, per_device(): lax.all_to_all(packed.reshape(FRONT, SLOTS, SHOTS + 128), front, 0, 0, ti...  7.6 us
    ppermute x1, starting transfers between devices, per_device(): other = lax.ppermute(gathered, 'core', swap)  6.96 us
    ppermute x1, starting transfers between devices, per_device(): other = lax.ppermute(send, 'core', swap)  4.72 us
    pallas_call x1, Pallas kernels, per_device(): pl.pallas_call(local_kernel, out_shape=(early, early), in_specs=[HBM] * 4...  4.57 us
  transfers between devices with their start and end apart: 3, of which 2 were waited for; matrix products, arithmetic and copies ran while one was open for 0% of the time, Pallas kernels for 6%

profile of v5, /device:TPU:1, one launch (start us, length us, event | category | flops | bytes accessed | tf_op | source)
XLA Modules:
  0.0 105.0 jit_solution(2143743608978048774)
XLA Ops:
  0.7 1.9 %shard_map.91 = f32[128,384]{1,0:T(8,128)} custom-call(s32[1,1]{1,0:T(1,128)} %bitcast.8.live_hbm, f32[64,256]{1,0:T(8,128)} %resid_hbm.1, s32[1,64]{1,0:T(1,128)} %bitcast.15, s32[1,64]{1,0:T(1,128)} %bitcast.16), custom_call_target="tpu_custom_call" | custom-call | tf_op jit(solution)/shard_map/pallas_call | solution.py:326
  2.5 7.6 %all-to-all-start = ((f32[16,8,384]{2,1,0:T(8,128)}), f32[16,8,384]{2,1,0:T(8,128)S(1)}, u32[]{:S(2)}, u32[]{:S(2)}) async-start(f32[16,8,384]{2,1,0:T(8,128)} %bitcast.14), calls=%async_computation | async-start | bytes 393216 | tf_op jit(solution)/shard_map/all_to_all | solution.py:341
  10.1 0.0 copy-start.2
  10.1 0.0 copy-start.3
  10.2 0.0 copy-start.4
  10.2 4.6 %shard_map.93 = (f32[1152,128]{1,0:T(8,128)}, f32[1152,128]{1,0:T(8,128)}) custom-call(bf16[4,384,256]{2,1,0:T(8,128)(2,1)} %rhs_ref.3, bf16[4,384,384]{2,1,0:T(8,128)(2,1)} %dinv_ref.2, bf16[3,384,128]{2,1,0:T(8,128)(2,1)} %u_ref.1, bf16[3,384,128]{2,1,0:T(8,128)(2,1)} %v_ref.3), custom_call_target="tpu_custom_call" | custom-call | flops 20000000000 | bytes 8000000 | tf_op jit(solution)/shard_map/pallas_call | solution.py:346
  14.7 4.7 %collective-permute-start = (f32[1152,128]{1,0:T(8,128)}, f32[1152,128]{1,0:T(8,128)S(1)}, u32[]{:S(2)}, u32[]{:S(2)}) collective-permute-start(f32[1152,128]{1,0:T(8,128)} %get-tuple-element.21), channel_id=1, source_target_pairs={{0,16},{16,0},{1,17},{17,1},{2,18},{18,2},{3,19},{19,3},{4,20},{20... | collective-permute-start | bytes 1769480 | tf_op jit(solution)/shard_map/ppermute | solution.py:365
  19.5 0.0 all-to-all-done
  19.5 0.0 copy-done.2
  19.5 0.0 copy-done.3
  19.5 0.0 copy-start
  19.5 0.9 shard_map.92
  20.4 0.8 collective-permute-done.other_ref
  21.3 0.1 shard_map.94
  21.4 19.2 %all_to_all.25.pieces_ref = f32[16,88,128]{2,1,0:T(8,128)S(1)} all-to-all(f32[16,88,128]{2,1,0:T(8,128)S(1)} %bitcast.11), channel_id=1, replica_groups=mesh['zh'=4,'zl'=4,'core'=2,'x'=4,'y'=4] {'x','y'}, dimensions={0} | all-to-all | bytes 1441792 | tf_op jit(solution)/shard_map/all_to_all | solution.py:402
  40.6 11.6 %all_to_all.26.pieces_ref = f32[8,32,128]{2,1,0:T(8,128)S(1)} all-to-all(f32[8,32,128]{2,1,0:T(8,128)S(1)} %shard_map.95), channel_id=1, replica_groups=mesh['zh'=4,'zl'=4,'core'=2,'x'=4,'y'=4] {'zl','core'}, dimensions={0} | all-to-all | bytes 262144 | tf_op jit(solution)/shard_map/all_to_all | solution.py:410
  52.2 24.0 %all_to_all.27.cross_ref = f32[16,16,128]{2,1,0:T(8,128)S(1)} all-to-all(f32[16,16,128]{2,1,0:T(8,128)S(1)} %get-tuple-element.23), channel_id=1, replica_groups=mesh['zh'=4,'zl'=4,'core'=2,'x'=4,'y'=4] {'zh','zl'}, dimensions={0} | all-to-all | bytes 262144 | tf_op jit(solution)/shard_map/all_to_all | solution.py:421
  76.2 0.1 shard_map.97
  76.3 16.3 %all_to_all.28 = f32[16,128,128]{2,1,0:T(8,128)S(1)} all-to-all(f32[16,128,128]{2,1,0:T(8,128)S(1)} %shard_map.97), channel_id=1, replica_groups=mesh['zh'=4,'zl'=4,'core'=2,'x'=4,'y'=4] {'x','y'}, dimensions={0} | all-to-all | bytes 2097152 | tf_op jit(solution)/shard_map/all_to_all | solution.py:429
  92.6 7.0 %collective-permute-start.1 = (f32[2048,128]{1,0:T(8,128)S(1)}, f32[2048,128]{1,0:T(8,128)S(1)}, u32[]{:S(2)}, u32[]{:S(2)}) collective-permute-start(f32[2048,128]{1,0:T(8,128)S(1)} %bitcast.9), channel_id=1, source_target_pairs={{0,16},{16,0},{1,17},{17,1},{2,18},{18,2},{3,19},{19,3},{4,20},{20... | collective-permute-start | bytes 3145736 | tf_op jit(solution)/shard_map/ppermute | solution.py:430
  99.6 0.9 shard_map.98
  100.5 1.3 %collective-permute-done.1.other_ref = f32[2048,128]{1,0:T(8,128)S(1)} collective-permute-done((f32[2048,128]{1,0:T(8,128)S(1)}, f32[2048,128]{1,0:T(8,128)S(1)}, u32[]{:S(2)}, u32[]{:S(2)}) %collective-permute-start.1) | collective-permute-done | bytes 1048608 | tf_op jit(solution)/shard_map/ppermute | solution.py:430
  101.8 0.0 copy-done.1
  101.8 3.2 %shard_map.99 = f32[4,384,256]{2,1,0:T(8,128)} custom-call(s32[1,3]{1,0:T(1,128)S(1)} %bitcast.13, f32[2048,128]{1,0:T(8,128)S(1)} %bitcast.10, f32[2048,128]{1,0:T(8,128)S(1)} %collective-permute-done.1.other_ref, f32[3,384,256]{2,1,0:T(8,128)S(1)} %get-tuple-element.26.own_ref, f32[384,256]{1,0:T(8,128)S(1)} %get-tuple-element.27.forward_ref, ...), custom_call_target="tpu_custom_call" | custom-call | tf_op jit(solution)/shard_map/pallas_call | solution.py:432
  (7 shorter events, 0.1 us)
Async XLA Ops:
  2.5 17.0 %all-to-all-start = ((f32[16,8,384]{2,1,0:T(8,128)}), f32[16,8,384]{2,1,0:T(8,128)S(1)}, u32[]{:S(2)}, u32[]{:S(2)}) async-start(f32[16,8,384]{2,1,0:T(8,128)} %bitcast.14), calls=%async_computation | async-start | bytes 393216 | tf_op jit(solution)/shard_map/all_to_all | solution.py:341
  10.1 9.4 %copy-start.2 = (bf16[4,384,384]{2,1,0:T(8,128)(2,1)S(1)}, bf16[4,384,384]{2,1,0:T(8,128)(2,1)}, u32[]{:S(2)}) copy-start(bf16[4,384,384]{2,1,0:T(8,128)(2,1)} %dinv_ref.2) | copy-start | bytes 3538948
  10.1 9.4 %copy-start.3 = (bf16[4,384,256]{2,1,0:T(8,128)(2,1)S(1)}, bf16[4,384,256]{2,1,0:T(8,128)(2,1)}, u32[]{:S(2)}) copy-start(bf16[4,384,256]{2,1,0:T(8,128)(2,1)} %rhs_ref.3) | copy-start | bytes 2359300
  10.2 9.4 %copy-start.4 = (bf16[3,384,128]{2,1,0:T(8,128)(2,1)S(1)}, bf16[3,384,128]{2,1,0:T(8,128)(2,1)}, u32[]{:S(2)}) copy-start(bf16[3,384,128]{2,1,0:T(8,128)(2,1)} %v_ref.3) | copy-start | bytes 884740
  14.7 6.5 %collective-permute-start = (f32[1152,128]{1,0:T(8,128)}, f32[1152,128]{1,0:T(8,128)S(1)}, u32[]{:S(2)}, u32[]{:S(2)}) collective-permute-start(f32[1152,128]{1,0:T(8,128)} %get-tuple-element.21), channel_id=1, source_target_pairs={{0,16},{16,0},{1,17},{17,1},{2,18},{18,2},{3,19},{19,3},{4,20},{20... | collective-permute-start | bytes 1769480 | tf_op jit(solution)/shard_map/ppermute | solution.py:365
  19.5 1.8 %copy-start = (f32[1152,128]{1,0:T(8,128)S(1)}, f32[1152,128]{1,0:T(8,128)}, u32[]{:S(2)}) copy-start(f32[1152,128]{1,0:T(8,128)} %get-tuple-element.20.mine_ref) | copy-start | bytes 1769476
  76.2 23.3 %copy-start.5 = (bf16[3,384,128]{2,1,0:T(8,128)(2,1)S(1)}, bf16[3,384,128]{2,1,0:T(8,128)(2,1)}, u32[]{:S(2)}) copy-start(bf16[3,384,128]{2,1,0:T(8,128)(2,1)} %u_ref.1) | copy-start | bytes 884740
  92.6 9.2 %copy-start.1 = (s32[3]{0:T(128)S(1)}, s32[3]{0:T(128)}, u32[]{:S(2)}) copy-start(s32[3]{0:T(128)} %param.13) | copy-start | bytes 40
  92.6 9.2 %collective-permute-start.1 = (f32[2048,128]{1,0:T(8,128)S(1)}, f32[2048,128]{1,0:T(8,128)S(1)}, u32[]{:S(2)}, u32[]{:S(2)}) collective-permute-start(f32[2048,128]{1,0:T(8,128)S(1)} %bitcast.9), channel_id=1, source_target_pairs={{0,16},{16,0},{1,17},{17,1},{2,18},{18,2},{3,19},{19,3},{4,20},{20... | collective-permute-start | bytes 3145736 | tf_op jit(solution)/shard_map/ppermute | solution.py:430
